TPU v7x, 128 devices: a whole 4x4x4 slice. The times are simulated.
128 devices in a mesh: band: 16 (over y, z), shard: 8 (over x, core).
Axes of the slice: x: 4, y: 4, z: 4, core: 2. Of those that a mesh axis runs over, the one named last changes fastest.
Arguments:
- grid_input: bfloat16 [1024, 512, 474], P('band', 'shard'), may hold values from -6 to 6
- w_stem: bfloat16 [9, 474, 512], replicated, may hold values from -0.09375 to 0.09375
- b_stem: float32 [512], replicated, may hold values from -3 to 3
- w_edge: bfloat16 [512, 512], replicated, may hold values from -0.25 to 0.25
- w_node: bfloat16 [512, 512], replicated, may hold values from -0.25 to 0.25
- src_index: int32 [128, 128, 16], P(('band', 'shard')), may hold values from 0 to 1023
- dst_index: int32 [128, 128, 16], P(('band', 'shard')), may hold values from 0 to 319
- counts: int32 [128, 128], P(('band', 'shard')), may hold values from 0 to 16, as said below
- mesh_cotangent: bfloat16 [40960, 512], P(('band', 'shard')), may hold values from -0.119628906 to 0.119628906
Outputs:
- mesh_out: bfloat16 [40960, 512], P(('band', 'shard'))
- grad_stem: float32 [9, 474, 512], replicated
- grad_bias: float32 [512], replicated
- grad_edge: float32 [512, 512], replicated
- grad_node: float32 [512, 512], replicated
Inputs may be any that keep to these rules, and one draw needn't show every extreme that they name: counts[q, r] of the 16 slots of each block are used; 16 is reached, and some destination owner receives 16 from every sender.
All inputs are finite; a program needn't handle non-finite values.
Results may differ from a plain program's by a relative error of at most 0.0066.
Values may be sent and summed in bfloat16 or wider, within the bound.
No kernel may reach another device: no remote copies, remote signals or barrier semaphores. Data moves between devices by JAX's collectives and lax.ppermute only.
A program may use at most 128 MiB of HBM per device.

v0:
```python
import jax
import jax.numpy as jnp
from jax import lax
from jax.sharding import PartitionSpec as P


def passed_along(array, axis, by):
    size = lax.axis_size(axis)
    return lax.ppermute(array, axis, [(i, (i + by) % size) for i in range(size)])


def from_behind(array, axis, by):
    size = lax.axis_size(axis)
    pairs = [(i, i + by) for i in range(size) if 0 <= i + by < size]
    return lax.ppermute(array, axis, pairs)


def silu_grad(values):
    sigmoid = jax.nn.sigmoid(values)
    return sigmoid * (1.0 + values * (1.0 - sigmoid))


def inner_dot(first, second):
    return lax.dot_general(
        first, second, (((0,), (0,)), ((), ())), preferred_element_type=jnp.float32
    )


def right_dot(first, second):
    return lax.dot_general(
        first, second, (((1,), (1,)), ((), ())), preferred_element_type=jnp.float32
    )


def phase_taps(row_phase, col_phase):
    return [
        (row_tap, col_tap)
        for row_tap in range(3)
        for col_tap in range(3)
        if row_tap % 2 == row_phase and col_tap % 2 == col_phase
    ]


def shards(
    grid_input, w_stem, b_stem, w_edge, w_node, src_index, dst_index, counts, mesh_cotangent
):
    rows_here, cols_here, channels = grid_input.shape
    latent_width = w_edge.shape[0]
    band_count = lax.axis_size("band")
    device_count = band_count * lax.axis_size("shard")
    slot_count = src_index.shape[2]
    half_rows = rows_here // 2
    half_cols = cols_here // 2
    west_column = passed_along(grid_input[:, -1:, :], "shard", 1)
    widened = jnp.concatenate([west_column, grid_input], axis=1)
    north_row = from_behind(widened[-1:, :, :], "band", 1)
    extended = jnp.concatenate([north_row, widened], axis=0)
    extended = jnp.pad(extended, ((0, 1), (0, 1), (0, 0)))
    phased = extended.reshape(half_rows + 1, 2, half_cols + 1, 2, channels)
    phase_list = []
    for row_phase in range(2):
        for col_phase in range(2):
            phase_list.append((row_phase, col_phase, phased[:, row_phase, :, col_phase, :]))
    stem_pre = jnp.zeros((half_rows, half_cols, latent_width), jnp.float32)
    for row_phase, col_phase, piece in phase_list:
        taps = phase_taps(row_phase, col_phase)
        kernels = jnp.concatenate(
            [w_stem[3 * row_tap + col_tap] for row_tap, col_tap in taps], axis=1
        )
        product = jnp.einsum("ijc,cl->ijl", piece, kernels, preferred_element_type=jnp.float32)
        for order, (row_tap, col_tap) in enumerate(taps):
            row_start = row_tap // 2
            col_start = col_tap // 2
            stem_pre = (
                stem_pre
                + product[
                    row_start : row_start + half_rows,
                    col_start : col_start + half_cols,
                    order * latent_width : (order + 1) * latent_width,
                ]
            )
    stem_pre = (stem_pre + b_stem).reshape(-1, latent_width)
    latent = jax.nn.silu(stem_pre).astype(jnp.bfloat16)
    points = latent.shape[0]
    flat_src = src_index.reshape(device_count, slot_count)
    slot_live = jnp.arange(slot_count, dtype=jnp.int32)[None, :] < counts.reshape(device_count, 1)
    taken = jnp.take(latent, flat_src, axis=0)
    outgoing = jnp.where(slot_live[:, :, None], taken, jnp.zeros_like(taken))
    incoming = lax.all_to_all(outgoing, ("band", "shard"), split_axis=0, concat_axis=0, tiled=True)
    projected = jnp.einsum("qcl,lk->qck", incoming, w_edge, preferred_element_type=jnp.float32)
    edge_pre = projected
    edge_pre = edge_pre.reshape(-1, latent_width)
    arrived_flat = incoming.reshape(-1, latent_width)
    messages = jax.nn.silu(edge_pre).astype(jnp.bfloat16)
    node_total = mesh_cotangent.shape[0]
    dst_flat = dst_index.reshape(1, -1)
    onehot = (jnp.arange(node_total, dtype=jnp.int32)[:, None] == dst_flat).astype(jnp.bfloat16)
    aggregate = jnp.dot(onehot, messages, preferred_element_type=jnp.float32).astype(jnp.bfloat16)
    mesh_out = jnp.dot(aggregate, w_node, preferred_element_type=jnp.float32).astype(jnp.bfloat16)
    grad_agg = right_dot(mesh_cotangent, w_node).astype(jnp.bfloat16)
    grad_node = inner_dot(aggregate, mesh_cotangent)
    grad_msg = inner_dot(onehot, grad_agg)
    grad_pre = (grad_msg * silu_grad(edge_pre)).astype(jnp.bfloat16)
    grad_edge = inner_dot(arrived_flat, grad_pre)
    grad_rows = (
        right_dot(grad_pre, w_edge)
        .astype(jnp.bfloat16)
        .reshape(device_count, slot_count, latent_width)
    )
    returned = lax.all_to_all(grad_rows, ("band", "shard"), split_axis=0, concat_axis=0, tiled=True)
    returned = returned.reshape(-1, latent_width)
    source_pick = (
        jnp.arange(points, dtype=jnp.int32)[:, None] == flat_src.reshape(1, -1)
    ) & slot_live.reshape(1, -1)
    grad_latent = jnp.dot(
        source_pick.astype(jnp.bfloat16), returned, preferred_element_type=jnp.float32
    )
    grad_stemout = (grad_latent * silu_grad(stem_pre)).astype(jnp.bfloat16)
    grad_grid = grad_stemout.reshape(half_rows, half_cols, latent_width)
    tap_grads = {}
    for row_phase, col_phase, piece in phase_list:
        taps = phase_taps(row_phase, col_phase)
        placed = [
            jnp.pad(
                grad_grid,
                ((row_tap // 2, 1 - row_tap // 2), (col_tap // 2, 1 - col_tap // 2), (0, 0)),
            )
            for row_tap, col_tap in taps
        ]
        stacked = jnp.concatenate(placed, axis=2)
        contracted = jnp.einsum("ijc,ijl->cl", piece, stacked, preferred_element_type=jnp.float32)
        for order, (row_tap, col_tap) in enumerate(taps):
            tap_grads[3 * row_tap + col_tap] = contracted[
                :, order * latent_width : (order + 1) * latent_width
            ]
    local_stem = jnp.stack([tap_grads[number] for number in range(9)], axis=0)
    local_bias = jnp.sum(grad_stemout.astype(jnp.float32), axis=0)
    summed = lax.psum((local_stem, local_bias, grad_edge, grad_node), ("band", "shard"))
    return (mesh_out, summed[0], summed[1], summed[2], summed[3])


def solution(mesh):
    in_specs = (
        P("band", "shard", None),
        P(),
        P(),
        P(),
        P(),
        P(("band", "shard"), None, None),
        P(("band", "shard"), None, None),
        P(("band", "shard"), None),
        P(("band", "shard"), None),
    )
    out_specs = (P(("band", "shard"), None), P(), P(), P(), P())
    return jax.shard_map(shards, mesh=mesh, in_specs=in_specs, out_specs=out_specs, check_vma=False)
```

profile of v0, /device:TPU:1, one launch (start us, length us, event | category | flops | bytes accessed | tf_op | source)
XLA Modules:
  0.0 367.0 jit_solution(10474201099725594925)
XLA Ops:
  8.4 2.6 collective-permute-start
  12.7 3.5 slice_bitcast_fusion.15
  16.3 3.5 collective-permute-start.1
  21.7 7.8 %fusion.21 = bf16[66,66,474]{2,1,0:T(8,128)(2,1)} fusion(bf16[1,65,474]{2,1,0:T(8,128)(2,1)S(1)} %collective-permute-done.1, bf16[64,64,474]{2,1,0:T(8,128)(2,1)} %param.9, bf16[64,1,474]{2,1,0:T(2,128)(2,1)S(1)} %collective-permute-done), kind=kLoop, calls=%fused_computation.24 | loop fusion | flops 30971160 | bytes 8134788 | tf_op jit(solution)/shard_map/concatenate | solution.py:57
  29.5 10.1 %reshape.115 = bf16[33,2,33,2,474]{4,3,2,1,0:T(2,128)(2,1)} reshape(bf16[66,66,474]{2,1,0:T(8,128)(2,1)} %fusion.21) | data formatting | bytes 8258976 | tf_op jit(solution)/shard_map/reshape | solution.py:59
  39.6 9.4 %fusion.95 = (bf16[33,1,33,1,474]{4,3,2,1,0:T(2,128)(2,1)S(1)}, bf16[33,1,33,1,474]{4,3,2,1,0:T(2,128)(2,1)S(1)}, bf16[33,1,33,1,474]{4,3,2,1,0:T(2,128)(2,1)S(1)}, bf16[33,1,33,1,474]{4,3,2,1,0:T(2,128)(2,1)S(1)}) fusion(bf16[33,2,33,2,474]{4,3,2,1,0:T(2,128)(2,1)} %reshape.115), kind=kLoop, calls=%fused_computation.145 | loop fusion | bytes 8258976 | tf_op jit(solution)/shard_map/slice | solution.py:63
  53.0 3.0 fusion.52
  56.0 2.9 fusion.43
  60.9 9.4 %gather_fusion = bf16[2048,512]{1,0:T(8,128)(2,1)} fusion(bf16[1024,512]{1,0:T(8,128)(2,1)S(1)} %fusion.47, s32[2048]{0:T(1024)S(1)} %broadcast_clamp_fusion), kind=kCustom, calls=%fused_computation | custom fusion | bytes 4202496 | tf_op jit(solution)/shard_map/jit(_take)/gather | solution.py:87
  70.3 2.9 select_select_fusion
  73.1 10.2 %all-to-all-start = ((bf16[128,16,512]{2,1,0:T(8,128)(2,1)}), bf16[128,16,512]{2,1,0:T(8,128)(2,1)S(1)}, u32[]{:S(2)}, u32[]{:S(2)}) async-start(bf16[128,16,512]{2,1,0:T(8,128)(2,1)} %select_select_fusion), calls=%async_computation | async-start | bytes 4194304 | tf_op jit(solution)/shard_map/all_to_all | solution.py:89
  83.6 30.3 %all-to-all-done = bf16[128,16,512]{2,1,0:T(8,128)(2,1)S(1)} async-done(((bf16[128,16,512]{2,1,0:T(8,128)(2,1)}), bf16[128,16,512]{2,1,0:T(8,128)(2,1)S(1)}, u32[]{:S(2)}, u32[]{:S(2)}) %all-to-all-start) | async-done | bytes 2097184 | tf_op jit(solution)/shard_map/all_to_all | solution.py:89
  113.9 3.3 fusion.82
  117.2 5.6 %fusion.30 = bf16[2048,512]{1,0:T(8,128)(2,1)} fusion(f32[128,16,512]{2,1,0:T(8,128)} %fusion.82, s32[2048]{0:T(1024)S(1)} %eq.31, bf16[320,512]{1,0:T(8,128)(2,1)S(1)} %copy-done.18, bf16[512,512]{1,0:T(8,128)(2,1)S(1)} %copy-done.14), kind=kOutput, calls=%fused_computation.36 | convolution fusion | flops 849117184 | bytes 7151616 | tf_op jit(solution)/shard_map/dot_general | solution.py:24
  122.7 4.2 %convolution_convert_fusion = bf16[2048,512]{1,0:T(8,128)(2,1)} fusion(bf16[2048,512]{1,0:T(8,128)(2,1)} %fusion.30, bf16[512,512]{1,0:T(8,128)(2,1)S(1)} %copy-done), kind=kOutput, calls=%fused_computation.42 | convolution fusion | flops 1074790400 | bytes 4718592 | tf_op jit(solution)/shard_map/dot_general | solution.py:30
  126.9 5.4 %all-to-all-start.1 = ((bf16[128,16,512]{2,1,0:T(8,128)(2,1)}), bf16[128,16,512]{2,1,0:T(8,128)(2,1)}, u32[]{:S(2)}, u32[]{:S(2)}) async-start(bf16[128,16,512]{2,1,0:T(8,128)(2,1)} %bitcast.168), calls=%async_computation.1 | async-start | bytes 4194304 | tf_op jit(solution)/shard_map/all_to_all | solution.py:110
  132.7 3.3 fusion.26
  138.3 2.2 fusion.98
  140.5 22.2 %all-to-all-done.1 = bf16[128,16,512]{2,1,0:T(8,128)(2,1)} async-done(((bf16[128,16,512]{2,1,0:T(8,128)(2,1)}), bf16[128,16,512]{2,1,0:T(8,128)(2,1)}, u32[]{:S(2)}, u32[]{:S(2)}) %all-to-all-start.1) | async-done | bytes 2097184 | tf_op jit(solution)/shard_map/all_to_all | solution.py:110
  162.7 5.2 %convert_reduce_fusion = (f32[512]{0:T(512)S(1)}, bf16[1024,512]{1,0:T(8,128)(2,1)S(1)}) fusion(f32[32,32,512]{2,1,0:T(8,128)} %copy-done.9, bf16[2048,512]{1,0:T(8,128)(2,1)} %bitcast.25, s32[2048]{0:T(1024)S(1)} %eq.35, pred[2048]{0:T(1024)(128)(4,1)S(1)} %lt.55), kind=kOutput, calls=%fused_computation.70 | convolution fusion | flops 2157444608 | bytes 5255168 | tf_op jit(solution)/shard_map/dot_general | solution.py:115
  173.0 3.6 fusion.33
  187.8 62.8 %psum.29 = f32[512]{0:T(512)} all-reduce(f32[512]{0:T(512)S(1)} %get-tuple-element.23), channel_id=1, replica_groups=mesh['band'=16,'shard'=8] {'band','shard'}, use_global_device_ids=true, to_apply=%region_2.3 | all-reduce | flops 512 | bytes 4096 | tf_op jit(solution)/shard_map/psum | solution.py:138
  250.6 98.7 %all-reduce.8.cloned.1.call-done = (f32[9,474,512]{2,1,0:T(8,128)}, f32[512,512]{1,0:T(8,128)}, f32[512,512]{1,0:T(8,128)}) async-done(((f32[9,474,512]{2,1,0:T(8,128)}, f32[512,512]{1,0:T(8,128)}, f32[512,512]{1,0:T(8,128)}), (f32[9,474,512]{2,1,0:T(8,128)}, f32[512,512]{1,0:T(8,128)}, f32[512,512]{1,0:T(8,128)})) %all-reduce.8.cloned.1.call-update) | async-done | bytes 10833936 | tf_op jit(solution)/shard_map/psum | solution.py:138
  349.4 8.2 %copy.63 = f32[9,474,512]{2,1,0:T(8,128)} copy(f32[9,474,512]{2,1,0:T(8,128)} %get-tuple-element.26) | data formatting | bytes 17473536
  (85 shorter events, 32.2 us)
Async XLA Ops:
  7.2 106.7 %copy-start = (bf16[512,512]{1,0:T(8,128)(2,1)S(1)}, bf16[512,512]{1,0:T(8,128)(2,1)}, u32[]{:S(2)}) copy-start(bf16[512,512]{1,0:T(8,128)(2,1)} %param.12) | copy-start | bytes 1572868
  8.4 7.8 %collective-permute-start = (bf16[64,1,474]{2,1,0:T(2,128)(2,1)S(1)}, bf16[64,1,474]{2,1,0:T(2,128)(2,1)S(1)}, u32[]{:S(2)}, u32[]{:S(2)}) collective-permute-start(bf16[64,1,474]{2,1,0:T(2,128)(2,1)S(1)} %slice.96), channel_id=1, source_target_pairs={{0,1},{1,2},{2,3},{3,4},{4,5},{5,6},{6,7},{7,0},{8,9},{9,10},{10,1... | collective-permute-start | bytes 182024 | tf_op jit(solution)/shard_map/ppermute | solution.py:9
  12.7 3.6 copy-start.2
  16.2 3.6 copy-start.19
  16.3 5.4 %collective-permute-start.1 = (bf16[1,65,474]{2,1,0:T(8,128)(2,1)S(1)}, bf16[1,65,474]{2,1,0:T(8,128)(2,1)S(1)}, u32[]{:S(2)}, u32[]{:S(2)}) collective-permute-start(bf16[1,65,474]{2,1,0:T(8,128)(2,1)S(1)} %pad_maximum_fusion.8), channel_id=1, source_target_pairs={{0,8},{8,16},{16,24},{24,32},{32,40},{40,48},{48,56},{56,64},{64,7... | collective-permute-start | bytes 184868 | tf_op jit(solution)/shard_map/ppermute | solution.py:15
  49.0 2.0 copy-start.5
  49.1 2.0 copy-start.3
  49.1 3.6 copy-start.7
  49.5 6.5 %copy-start.10 = (bf16[33,1,33,1,474]{4,2,0,3,1:T(8,128)(2,1)}, bf16[33,1,33,1,474]{4,2,0,3,1:T(8,128)(2,1)S(1)}, u32[]{:S(2)}) copy-start(bf16[33,1,33,1,474]{4,2,0,3,1:T(8,128)(2,1)S(1)} %copy.51) | copy-start | bytes 3097120
  51.1 1.7 copy-start.16
  51.1 1.9 copy-start.17
  53.0 3.0 copy-start.21
  73.1 10.2 %copy-start.20 = (s32[1,128,16]{1,2,0:T(8,128)S(1)}, s32[1,128,16]{1,2,0:T(8,128)}, u32[]{:S(2)}) copy-start(s32[1,128,16]{1,2,0:T(8,128)} %param.15) | copy-start | bytes 24580
  73.1 40.8 %all-to-all-start = ((bf16[128,16,512]{2,1,0:T(8,128)(2,1)}), bf16[128,16,512]{2,1,0:T(8,128)(2,1)S(1)}, u32[]{:S(2)}, u32[]{:S(2)}) async-start(bf16[128,16,512]{2,1,0:T(8,128)(2,1)} %select_select_fusion), calls=%async_computation | async-start | bytes 4194304 | tf_op jit(solution)/shard_map/all_to_all | solution.py:89
  83.6 33.6 %copy-start.14 = (bf16[512,512]{1,0:T(8,128)(2,1)S(1)}, bf16[512,512]{1,0:T(8,128)(2,1)}, u32[]{:S(2)}) copy-start(bf16[512,512]{1,0:T(8,128)(2,1)} %param.13) | copy-start | bytes 1572868
  83.6 33.6 %copy-start.18 = (bf16[320,512]{1,0:T(8,128)(2,1)S(1)}, bf16[320,512]{1,0:T(8,128)(2,1)}, u32[]{:S(2)}) copy-start(bf16[320,512]{1,0:T(8,128)(2,1)} %param.17) | copy-start | bytes 983044
  126.9 35.7 %all-to-all-start.1 = ((bf16[128,16,512]{2,1,0:T(8,128)(2,1)}), bf16[128,16,512]{2,1,0:T(8,128)(2,1)}, u32[]{:S(2)}, u32[]{:S(2)}) async-start(bf16[128,16,512]{2,1,0:T(8,128)(2,1)} %bitcast.168), calls=%async_computation.1 | async-start | bytes 4194304 | tf_op jit(solution)/shard_map/all_to_all | solution.py:110
  132.3 217.0 %all-reduce.8.cloned.1.call-start = ((), (), s32[]{:S(2)}) async-start(), calls=%async_computation.2 | async-start | bytes 21889024 | tf_op jit(solution)/shard_map/psum | solution.py:138
  136.0 2.3 copy-start.22
  169.4 1.8 copy-start.4
  171.2 1.8 copy-start.8
  178.7 2.0 copy-start.11
  349.4 8.2 %copy-start.13 = (f32[512,512]{1,0:T(8,128)S(1)}, f32[512,512]{1,0:T(8,128)}, u32[]{:S(2)}) copy-start(f32[512,512]{1,0:T(8,128)} %get-tuple-element.28) | copy-start | bytes 3145732
  349.4 10.8 %copy-start.1 = (bf16[512,512]{1,0:T(8,128)(2,1)S(1)}, bf16[512,512]{1,0:T(8,128)(2,1)}, u32[]{:S(2)}) copy-start(bf16[512,512]{1,0:T(8,128)(2,1)} %param.12) | copy-start | bytes 1572868
  (4 other events, 6.2 us)
Sparse Core Ops, SparseCore 0:
  186.9 162.4 all-reduce.7
where the time goes:
time: 368 us; the launch traced here: 367 us
  waiting for transfers between devices  153 us (42%)
  blocking collectives  62.8 us (17%)
  local copies, waits for them, and re-layouts  57.2 us (16%)
  matrix products  41.8 us (11%)
  starting transfers between devices  21.9 us (6%)
  other arithmetic  16 us (4%)
  between operations  14.4 us (4%)
    psum x1, waiting for transfers between devices, shards(): lax.psum((local_stem, local_bias, grad_edge, grad_node), ('band', 'shard'))  98.7 us
    psum x1, blocking collectives, shards(): lax.psum((local_stem, local_bias, grad_edge, grad_node), ('band', 'shard'))  62.8 us
    all_to_all x1, waiting for transfers between devices, shards(): lax.all_to_all(outgoing, ('band', 'shard'), split_axis=0, concat_axis=0,...  30.3 us
    all_to_all x1, waiting for transfers between devices, shards(): lax.all_to_all(grad_rows, ('band', 'shard'), split_axis=0, concat_axis=0,...  22.2 us
    unnamed x59, local copies, waits for them, and re-layouts  21.1 us
    all_to_all x1, starting transfers between devices, shards(): lax.all_to_all(outgoing, ('band', 'shard'), split_axis=0, concat_axis=0,...  10.2 us
    reshape x1, local copies, waits for them, and re-layouts, shards(): phased = extended.reshape(half_rows + 1, 2, half_cols + 1, 2, channels)  10.1 us
    slice x1, local copies, waits for them, and re-layouts, shards(): phased[:, row_phase, :, col_phase, :]  9.44 us
  transfers between devices with their start and end apart: 5, of which 4 were waited for; matrix products, arithmetic and copies ran while one was open for 4% of the time, Pallas kernels for 0%

commit v1 on v0

v1 whole, which is shorter than its diff:
```python
import functools

import jax
import jax.numpy as jnp
from jax import lax
from jax.experimental import pallas as pl
from jax.experimental.pallas import tpu as pltpu
from jax.sharding import Mesh, PartitionSpec as P

CHIPS = ("band", "chip")
EVERY = ("band", "chip", "core")
TAPS = 9
VMEM_LIMIT = 52 * 1024 * 1024


def f32_dot(first, second):
    return jnp.dot(first, second, preferred_element_type=jnp.float32)


def inner_dot(first, second):
    return lax.dot_general(
        first, second, (((0,), (0,)), ((), ())), preferred_element_type=jnp.float32
    )


def right_dot(first, second):
    return lax.dot_general(
        first, second, (((1,), (1,)), ((), ())), preferred_element_type=jnp.float32
    )


def core_swap(array):
    return lax.ppermute(array, "core", [(0, 1), (1, 0)])


def whole(memory=pltpu.VMEM):
    return pl.BlockSpec(memory_space=memory)


def params(**more):
    return pltpu.CompilerParams(vmem_limit_bytes=VMEM_LIMIT, **more)


def column_picker(image_rows, cols, parts):
    half = cols // 2
    shape = (3 * image_rows * half, image_rows * cols)
    out = lax.broadcasted_iota(jnp.int32, shape, 0)
    inside = lax.broadcasted_iota(jnp.int32, shape, 1)
    per_tap = image_rows * half
    tap = out // per_tap
    rest = out - tap * per_tap
    line = rest // half
    col = 2 * (rest - line * half) + tap - 1
    if parts == 2:
        pairs = image_rows // 2
        parity = line // pairs
        line = 2 * (line - parity * pairs) + parity
    hit = (col >= 0) & (inside == line * cols + col)
    return jnp.where(hit, 1.0, 0.0).astype(jnp.bfloat16)


def stem_kernel(
    grid_hbm, west_ref, north_ref, corner_ref, picker_ref, north_picker_ref, w_hbm, bias_ref,
    source_ref, even_hbm, odd_hbm, slope_ref, out_ref,
    grid, weights, even, odd, latent, in_sems, w_sem, out_sems,
):
    rows, cols, channels = grid.shape
    half_rows, half_cols = rows // 2, cols // 2
    width = even.shape[-1]
    chunks = in_sems.shape[0]
    per_chunk = rows // chunks

    def load(chunk):
        part = pl.ds(chunk * per_chunk, per_chunk)
        return pltpu.make_async_copy(grid_hbm.at[part], grid.at[part], in_sems.at[chunk])

    for chunk in range(chunks):
        load(chunk).start()
    w_copy = pltpu.make_async_copy(w_hbm, weights, w_sem)
    w_copy.start()

    tail = width - 128
    even[:, :, :, tail:] = jnp.zeros((3, half_rows, half_cols, 128), jnp.bfloat16)
    odd[:, :, :, tail:] = jnp.zeros((3, half_rows + 1, half_cols, 128), jnp.bfloat16)
    picker = picker_ref[...]
    north = f32_dot(north_picker_ref[...], north_ref[0]).astype(jnp.bfloat16)
    for tap in range(3):
        odd[tap, 0, :, :channels] = north[tap * half_cols : (tap + 1) * half_cols]

    for chunk in range(chunks):
        load(chunk).wait()

        @pl.loop(chunk * per_chunk // 4, (chunk + 1) * per_chunk // 4)
        def _(group):
            block = grid[pl.ds(4 * group, 4)].reshape(4 * cols, channels)
            picked = f32_dot(picker, block).astype(jnp.bfloat16)
            picked = picked.reshape(3, 2, 2, half_cols, channels)
            for tap in range(3):
                even[tap, pl.ds(2 * group, 2), :, :channels] = picked[tap, 0]
                odd[tap, pl.ds(2 * group + 1, 2), :, :channels] = picked[tap, 1]

    def patch(target, first, count, column):
        old = target[0, first : first + count, 0:16, :channels].astype(jnp.float32)
        line = lax.broadcasted_iota(jnp.int32, old.shape, 1)
        new = jnp.where(line == 0, column.astype(jnp.float32), old)
        target[0, first : first + count, 0:16, :channels] = new.astype(jnp.bfloat16)

    patch(even, 0, half_rows, west_ref[:, 0])
    patch(odd, 1, half_rows, west_ref[:, 1])
    patch(odd, 0, 1, corner_ref[...])
    even_copy = pltpu.make_async_copy(even, even_hbm, out_sems.at[0])
    odd_copy = pltpu.make_async_copy(odd, odd_hbm, out_sems.at[1])
    even_copy.start()
    odd_copy.start()

    w_copy.wait()
    tile_rows = 8
    tile = tile_rows * half_cols

    @pl.loop(0, half_rows // tile_rows)
    def _(step):
        first = step * tile_rows
        pieces = []
        for row_tap in range(3):
            for col_tap in range(3):
                if row_tap == 1:
                    piece = even[col_tap, pl.ds(first, tile_rows)]
                else:
                    piece = odd[col_tap, pl.ds(first + row_tap // 2, tile_rows)]
                pieces.append(piece.reshape(tile, width))
        pre = f32_dot(jnp.concatenate(pieces, axis=1), weights[...]) + bias_ref[...]
        sigmoid = jax.nn.sigmoid(pre)
        here = pl.ds(pl.multiple_of(step * tile, tile), tile)
        slope_ref[here] = sigmoid * (1.0 + pre * (1.0 - sigmoid))
        latent[here] = (pre * sigmoid).astype(jnp.bfloat16)

    points = latent.shape[0]
    slots = out_ref.shape[0]

    @pl.loop(0, slots // 256)
    def _(step):
        here = pl.ds(pl.multiple_of(step * 256, 256), 256)
        point = lax.broadcasted_iota(jnp.int32, (256, points), 1)
        pick = jnp.where(point == source_ref[here], 1.0, 0.0).astype(jnp.bfloat16)
        out_ref[here] = f32_dot(pick, latent[...]).astype(jnp.bfloat16)

    even_copy.wait()
    odd_copy.wait()


def flip_kernel(channels, even_ref, odd_ref, out_ref):
    number = pl.program_id(0)
    row_tap = number // 3
    col_tap = number % 3
    half_rows, half_cols, width = even_ref.shape[1:]

    def write(values):
        flipped = values.reshape(half_rows * half_cols, width).T
        line = lax.broadcasted_iota(jnp.int32, flipped.shape, 0)
        ones = (line == channels) & (number == 0)
        out_ref[0] = jnp.where(ones, 1.0, flipped.astype(jnp.float32)).astype(jnp.bfloat16)

    @pl.when(row_tap == 1)
    def _():
        write(even_ref[col_tap])

    @pl.when(row_tap != 1)
    def _():
        write(odd_ref[col_tap, pl.ds(row_tap // 2, half_rows)])


def edge_kernel(rows_ref, w_ref, dst_ref, agg_ref, back_ref, message_ref, grad_ref):
    nodes = agg_ref.shape[0]
    tile = rows_ref.shape[0]
    weights = w_ref[...]
    pre = f32_dot(rows_ref[...], weights)
    node = lax.broadcasted_iota(jnp.int32, (tile, nodes), 1)
    pick = jnp.where(node == dst_ref[...], 1.0, 0.0).astype(jnp.bfloat16)
    grad_msg = f32_dot(pick, agg_ref[...])
    sigmoid = jax.nn.sigmoid(pre)
    message_ref[...] = (pre * sigmoid).astype(jnp.bfloat16)
    grad_pre = (grad_msg * (sigmoid * (1.0 + pre * (1.0 - sigmoid)))).astype(jnp.bfloat16)
    grad_ref[...] = grad_pre
    back_ref[...] = right_dot(grad_pre, weights).astype(jnp.bfloat16)


def sent_kernel(
    half_ref, patches_ref, small_ref, returned_ref, source_ref, slope_ref, out_ref, stemout_ref
):
    number = pl.program_id(0)
    points, width = stemout_ref.shape
    slots = returned_ref.shape[0]
    half_width = out_ref.shape[-1]

    @pl.when(number == 0)
    def _():
        @pl.loop(0, points // 256)
        def _(step):
            first = pl.multiple_of(step * 256, 256)
            here = pl.ds(first, 256)
            point = lax.broadcasted_iota(jnp.int32, (256, slots), 0) + first
            pick = jnp.where(point == source_ref[...], 1.0, 0.0).astype(jnp.bfloat16)
            grad_latent = f32_dot(pick, returned_ref[...])
            stemout_ref[here] = (grad_latent * slope_ref[here]).astype(jnp.bfloat16)

    columns = pl.ds(pl.multiple_of(half_ref[0] * half_width, half_width), half_width)

    @pl.when(number < TAPS)
    def _():
        out_ref[0] = f32_dot(patches_ref[0], stemout_ref[:, columns]).astype(out_ref.dtype)

    @pl.when(number >= TAPS)
    def _():
        out_ref[0] = small_ref[0, :, columns].astype(out_ref.dtype)


def kept_kernel(half_ref, patches_ref, small_ref, stemout_ref, out_ref):
    number = pl.program_id(0)
    half_width = out_ref.shape[-1]
    columns = pl.ds(pl.multiple_of(half_ref[0] * half_width, half_width), half_width)

    @pl.when(number < TAPS)
    def _():
        out_ref[0] = f32_dot(patches_ref[0], stemout_ref[:, columns])

    @pl.when(number >= TAPS)
    def _():
        out_ref[0] = small_ref[0, :, columns]


def final_kernel(core_ref, mine_ref, other_ref, stem_ref, bias_ref, edge_ref, node_ref):
    number = pl.program_id(0)
    channels = stem_ref.shape[1]
    half_width = mine_ref.shape[-1]
    mine = mine_ref[0].astype(jnp.float32)
    other = other_ref[0].astype(jnp.float32)
    first = core_ref[0] == 0
    left = jnp.where(first, mine, other)
    right = jnp.where(first, other, mine)

    @pl.when(number < TAPS)
    def _():
        stem_ref[0, :, :half_width] = left[:channels]
        stem_ref[0, :, half_width:] = right[:channels]

    @pl.when(number == 0)
    def _():
        bias_ref[:, :half_width] = left[channels : channels + 1]
        bias_ref[:, half_width:] = right[channels : channels + 1]

    @pl.when(number == TAPS)
    def _():
        edge_ref[:, :half_width] = left
        edge_ref[:, half_width:] = right

    @pl.when(number == TAPS + 1)
    def _():
        node_ref[:, :half_width] = left
        node_ref[:, half_width:] = right


def shards(
    grid_input, w_stem, b_stem, w_edge, w_node, src_index, dst_index, counts, mesh_cotangent
):
    rows_here, cols_here, channels = grid_input.shape
    width = w_edge.shape[0]
    bands = lax.axis_size("band")
    columns = lax.axis_size("chip") * 2
    chips = bands * lax.axis_size("chip")
    core = lax.axis_index("core")
    device_count = 2 * chips
    slot_count = src_index.shape[2]
    slots = device_count * slot_count
    half_rows = rows_here // 2
    half_cols = cols_here // 2
    points = half_rows * half_cols
    half_width = width // 2
    node_total = mesh_cotangent.shape[0]
    bf16, f32 = jnp.bfloat16, jnp.float32

    west = lax.ppermute(
        grid_input[:, -1:, :], ("chip", "core"), [(i, (i + 1) % columns) for i in range(columns)]
    )
    north = lax.ppermute(grid_input[-1:], "band", [(i, i + 1) for i in range(bands - 1)])
    corner = lax.ppermute(
        grid_input[-1:, -1:],
        EVERY,
        [
            (i * columns + j, (i + 1) * columns + (j + 1) % columns)
            for i in range(bands - 1)
            for j in range(columns)
        ],
    )
    w_flat = jnp.pad(w_stem, ((0, 0), (0, width - channels), (0, 0))).reshape(TAPS * width, width)
    flat_src = src_index.reshape(device_count, slot_count)
    slot_live = jnp.arange(slot_count, dtype=jnp.int32)[None, :] < counts.reshape(device_count, 1)
    source = jnp.where(slot_live, flat_src, -1)

    even, odd, slope, outgoing = pl.pallas_call(
        stem_kernel,
        out_shape=(
            jax.ShapeDtypeStruct((3, half_rows, half_cols, width), bf16),
            jax.ShapeDtypeStruct((3, half_rows + 1, half_cols, width), bf16),
            jax.ShapeDtypeStruct((points, width), f32),
            jax.ShapeDtypeStruct((slots, width), bf16),
        ),
        in_specs=[
            whole(pl.ANY), whole(), whole(), whole(), whole(), whole(), whole(pl.ANY), whole(), whole(),
        ],
        out_specs=(whole(pl.ANY), whole(pl.ANY), whole(), whole()),
        scratch_shapes=[
            pltpu.VMEM((rows_here, cols_here, channels), bf16),
            pltpu.VMEM((TAPS * width, width), bf16),
            pltpu.VMEM((3, half_rows, half_cols, width), bf16),
            pltpu.VMEM((3, half_rows + 1, half_cols, width), bf16),
            pltpu.VMEM((points, width), bf16),
            pltpu.SemaphoreType.DMA((4,)),
            pltpu.SemaphoreType.DMA,
            pltpu.SemaphoreType.DMA((2,)),
        ],
        compiler_params=params(),
        name="stem",
    )(
        grid_input,
        west.reshape(half_rows, 2, 1, channels),
        north,
        corner,
        column_picker(4, cols_here, 2),
        column_picker(1, cols_here, 1),
        w_flat,
        b_stem.reshape(1, width),
        source.reshape(slots, 1),
    )

    incoming = lax.all_to_all(
        outgoing.reshape(device_count, slot_count, width), EVERY, split_axis=0, concat_axis=0, tiled=True
    )
    arrived = incoming.reshape(slots, width)

    patches = pl.pallas_call(
        functools.partial(flip_kernel, channels),
        grid=(TAPS,),
        out_shape=jax.ShapeDtypeStruct((TAPS, width, points), bf16),
        in_specs=[
            pl.BlockSpec((3, half_rows, half_cols, width), lambda t: (0, 0, 0, 0)),
            pl.BlockSpec((3, half_rows + 1, half_cols, width), lambda t: (0, 0, 0, 0)),
        ],
        out_specs=pl.BlockSpec((1, width, points), lambda t: (t, 0, 0)),
        compiler_params=params(),
        cost_estimate=pl.CostEstimate(flops=0, bytes_accessed=16 * 1024 * 1024, transcendentals=0),
        name="flip",
    )(even, odd)
    grad_agg = right_dot(mesh_cotangent, w_node).astype(bf16)
    dst_flat = dst_index.reshape(slots)

    tile = 256
    by_tile = pl.BlockSpec((tile, width), lambda i: (i, 0))
    back, messages, grad_pre = pl.pallas_call(
        edge_kernel,
        grid=(slots // tile,),
        out_shape=(jax.ShapeDtypeStruct((slots, width), bf16),) * 3,
        in_specs=[
            by_tile,
            pl.BlockSpec((width, width), lambda i: (0, 0)),
            pl.BlockSpec((tile, 1), lambda i: (i, 0)),
            pl.BlockSpec((node_total, width), lambda i: (0, 0)),
        ],
        out_specs=(by_tile,) * 3,
        compiler_params=params(),
        name="edge",
    )(arrived, w_edge, dst_flat.reshape(slots, 1), grad_agg)

    returned = lax.all_to_all(
        back.reshape(device_count, slot_count, width), EVERY, split_axis=0, concat_axis=0, tiled=True
    ).reshape(slots, width)

    node_ids = jnp.arange(node_total, dtype=jnp.int32)
    onehot = (node_ids[:, None] == dst_flat[None, :]).astype(bf16)
    aggregate = f32_dot(onehot, messages).astype(bf16)
    mesh_out = f32_dot(aggregate, w_node).astype(bf16)
    grad_node = inner_dot(aggregate, mesh_cotangent)
    grad_edge = inner_dot(arrived, grad_pre)
    small = jnp.stack([grad_edge, grad_node])

    blocks = TAPS + 2
    other_half = (1 - core).reshape(1)
    own_half = core.reshape(1)
    by_tap = pl.BlockSpec((1, width, points), lambda t, h: (jnp.minimum(t, TAPS - 1), 0, 0))
    by_small = pl.BlockSpec((1, width, width), lambda t, h: (jnp.maximum(t - TAPS, 0), 0, 0))
    by_block = pl.BlockSpec((1, width, half_width), lambda t, h: (t, 0, 0))
    fixed = lambda shape: pl.BlockSpec(shape, lambda t, h: (0,) * len(shape))
    sent, stemout = pl.pallas_call(
        sent_kernel,
        out_shape=(
            jax.ShapeDtypeStruct((blocks, width, half_width), bf16),
            jax.ShapeDtypeStruct((points, width), bf16),
        ),
        grid_spec=pltpu.PrefetchScalarGridSpec(
            num_scalar_prefetch=1,
            grid=(blocks,),
            in_specs=[
                by_tap, by_small, fixed((slots, width)), fixed((1, slots)), fixed((points, width)),
            ],
            out_specs=(by_block, fixed((points, width))),
        ),
        compiler_params=params(),
        name="sent_half",
    )(other_half, patches, small, returned, source.reshape(1, slots), slope)
    received = core_swap(sent)
    kept = pl.pallas_call(
        kept_kernel,
        out_shape=jax.ShapeDtypeStruct((blocks, width, half_width), f32),
        grid_spec=pltpu.PrefetchScalarGridSpec(
            num_scalar_prefetch=1,
            grid=(blocks,),
            in_specs=[by_tap, by_small, fixed((points, width))],
            out_specs=by_block,
        ),
        compiler_params=params(),
        cost_estimate=pl.CostEstimate(
            flops=2 * TAPS * width * points * half_width,
            bytes_accessed=20 * 1024 * 1024,
            transcendentals=0,
        ),
        name="kept_half",
    )(own_half, patches, small, stemout)

    chip_sum = (kept + received.astype(f32)).astype(bf16)
    chunk = blocks * width // chips
    pieces = lax.all_to_all(
        chip_sum.reshape(chips, chunk, half_width), CHIPS, split_axis=0, concat_axis=0, tiled=True
    )
    summed = jnp.sum(pieces.astype(f32), axis=0).astype(bf16)
    spread = jnp.broadcast_to(summed[None], (chips, chunk, half_width))
    gathered = lax.all_to_all(spread, CHIPS, split_axis=0, concat_axis=0, tiled=True)
    mine = gathered.reshape(blocks, width, half_width)
    other = core_swap(mine)

    grad_stem, grad_bias, out_edge, out_node = pl.pallas_call(
        final_kernel,
        out_shape=(
            jax.ShapeDtypeStruct((TAPS, channels, width), f32),
            jax.ShapeDtypeStruct((1, width), f32),
            jax.ShapeDtypeStruct((width, width), f32),
            jax.ShapeDtypeStruct((width, width), f32),
        ),
        grid_spec=pltpu.PrefetchScalarGridSpec(
            num_scalar_prefetch=1,
            grid=(blocks,),
            in_specs=[by_block, by_block],
            out_specs=(
                pl.BlockSpec((1, channels, width), lambda t, h: (jnp.minimum(t, TAPS - 1), 0, 0)),
                fixed((1, width)),
                fixed((width, width)),
                fixed((width, width)),
            ),
        ),
        compiler_params=params(),
        name="final",
    )(own_half, mine, other)
    return (mesh_out, grad_stem, grad_bias.reshape(width), out_edge, out_node)


def solution(mesh):
    bands, columns = mesh.devices.shape
    fine = Mesh(mesh.devices.reshape(bands, columns // 2, 2), EVERY)
    in_specs = (
        P("band", ("chip", "core"), None),
        P(),
        P(),
        P(),
        P(),
        P(EVERY, None, None),
        P(EVERY, None, None),
        P(EVERY, None),
        P(EVERY, None),
    )
    out_specs = (P(EVERY, None), P(), P(), P(), P())
    return jax.shard_map(shards, mesh=fine, in_specs=in_specs, out_specs=out_specs, check_vma=False)
```

time: 368 us -> 262 us (0.71)
  waiting for transfers between devices: 153 us -> 47.5 us
  Pallas kernels: 0 us -> 74.9 us
  local copies, waits for them, and re-layouts: 57.2 us -> 14 us
  matrix products: 41.8 us -> 5.58 us
  blocking collectives: 62.8 us -> 84.7 us
  between operations: 14.4 us -> 0.91 us
  other arithmetic: 16 us -> 6.7 us
  starting transfers between devices: 21.9 us -> 26.1 us
    psum x1 -> x0, waiting for transfers between devices: 98.7 us -> none  [shards(): lax.psum((local_stem, local_bias, grad_edge, grad_node), ('band', 'shard'))]
    all_to_all x0 -> x2, blocking collectives: none -> 84.7 us  [the longest x1 42.8 us: shards(): lax.all_to_all(chip_sum.reshape(chips, chunk, half_width), CHIPS, split_a...]
    pallas_call x0 -> x6, Pallas kernels: none -> 74.9 us  [the longest x1 18.2 us: shards(): pl.pallas_call(stem_kernel, out_shape=(jax.ShapeDtypeStruct((3, half_rows...]
    psum x1 -> x0, blocking collectives: 62.8 us -> none  [shards(): lax.psum((local_stem, local_bias, grad_edge, grad_node), ('band', 'shard'))]
    dot_general x12 -> x2, matrix products: 28.4 us -> 1.91 us  [f32_dot(): return jnp.dot(first, second, preferred_element_type=jnp.float32)]
    unnamed x59 -> x26, local copies, waits for them, and re-layouts: 21.1 us -> 4.12 us
    reshape x1 -> x2, local copies, waits for them, and re-layouts: 10.1 us -> 0.66 us  [shards(): flat_src = src_index.reshape(device_count, slot_count)]
    gather x1 -> x0, local copies, waits for them, and re-layouts: 9.39 us -> none  [shards(): taken = jnp.take(latent, flat_src, axis=0)]
  transfers between devices with their start and end apart: 5 -> 7, of which waited for: 4 -> 3; matrix products, arithmetic and copies ran while one was open for 4% -> 7% of each run, Pallas kernels for 0% -> 8%
where the time goes in v1:
time: 262 us; the launch traced here: 260 us
  blocking collectives  84.7 us (32%)
  Pallas kernels  74.9 us (29%)
  waiting for transfers between devices  47.5 us (18%)
  starting transfers between devices  26.1 us (10%)
  local copies, waits for them, and re-layouts  14 us (5%)
  other arithmetic  6.7 us (3%)
  matrix products  5.58 us (2%)
    all_to_all x1, blocking collectives, shards(): lax.all_to_all(chip_sum.reshape(chips, chunk, half_width), CHIPS, split_a...  42.8 us
    all_to_all x1, blocking collectives, shards(): lax.all_to_all(spread, CHIPS, split_axis=0, concat_axis=0, tiled=True)  41.9 us
    all_to_all x1, waiting for transfers between devices, shards(): lax.all_to_all(outgoing.reshape(device_count, slot_count, width), EVERY,...  29.1 us
    pallas_call x1, Pallas kernels, shards(): pl.pallas_call(stem_kernel, out_shape=(jax.ShapeDtypeStruct((3, half_rows...  18.2 us
    pallas_call x1, Pallas kernels, shards(): pl.pallas_call(sent_kernel, out_shape=(jax.ShapeDtypeStruct((blocks, widt...  15.6 us
    all_to_all x1, waiting for transfers between devices, shards(): lax.all_to_all(back.reshape(device_count, slot_count, width), EVERY, spli...  14.6 us
    pallas_call x1, Pallas kernels, shards(): pl.pallas_call(kept_kernel, out_shape=jax.ShapeDtypeStruct((blocks, width...  12.1 us
    pallas_call x1, Pallas kernels, shards(): pl.pallas_call(final_kernel, out_shape=(jax.ShapeDtypeStruct((TAPS, chann...  11 us
  transfers between devices with their start and end apart: 7, of which 3 were waited for; matrix products, arithmetic and copies ran while one was open for 7% of the time, Pallas kernels for 8%

profile of v1, /device:TPU:1, one launch (start us, length us, event | category | flops | bytes accessed | tf_op | source)
XLA Modules:
  0.0 260.5 jit_solution(16435587633815211703)
XLA Ops:
  1.4 5.8 %collective-permute-start.2 = (bf16[1,1,474]{2,1,0:T(2,128)(2,1)S(1)}, bf16[1,1,474]{2,1,0:T(2,128)(2,1)S(1)}, u32[]{:S(2)}, u32[]{:S(2)}) collective-permute-start(bf16[1,1,474]{2,1,0:T(2,128)(2,1)S(1)} %slice.11), channel_id=1, source_target_pairs={{0,9},{1,10},{2,11},{3,12},{4,13},{5,14},{6,15},{7,8},{8,17},{9,18... | collective-permute-start | bytes 2852 | tf_op jit(solution)/shard_map/ppermute | solution.py:285
  8.1 3.5 %collective-permute-start.1 = (bf16[1,64,474]{2,1,0:T(8,128)(2,1)S(1)}, bf16[1,64,474]{2,1,0:T(8,128)(2,1)S(1)}, u32[]{:S(2)}, u32[]{:S(2)}) collective-permute-start(bf16[1,64,474]{2,1,0:T(8,128)(2,1)S(1)} %slice.10), channel_id=1, source_target_pairs={{0,8},{8,16},{16,24},{24,32},{32,40},{40,48},{48,56},{56,64},{64,7... | collective-permute-start | bytes 182024 | tf_op jit(solution)/shard_map/ppermute | solution.py:284
  11.7 1.2 slice.9
  16.7 4.8 %pad.4 = bf16[9,512,512]{2,1,0:T(8,128)(2,1)} pad(bf16[9,474,512]{2,1,0:T(8,128)(2,1)} %param.10, bf16[]{:T(256)} %constant.85.clone.1), padding=0_0x0_38x0_0 | pad | bytes 9086978 | tf_op jit(solution)/shard_map/jit(_pad)/pad | solution.py:294
  21.5 18.2 %stem.1 = (bf16[3,32,32,512]{3,2,1,0:T(8,128)(2,1)}, bf16[3,33,32,512]{3,2,1,0:T(8,128)(2,1)}, f32[1024,512]{1,0:T(8,128)}, bf16[2048,512]{1,0:T(8,128)(2,1)}) custom-call(bf16[64,64,474]{2,1,0:T(8,128)(2,1)} %grid_hbm.1, bf16[32,2,1,474]{3,2,1,0:T(2,128)(2,1)S(1)} %bitcast.26, bf16[1,64,474]{2,1,0:T(8,128)(2,1)S(1)} %collective-permute-done.1.north_ref, ...), custom_call_target="tpu_custom_call" | custom-call | tf_op jit(solution)/shard_map/stem/pallas_call | solution.py:299
  39.7 8.5 %all-to-all-start = ((bf16[128,16,512]{2,1,0:T(8,128)(2,1)}), bf16[128,16,512]{2,1,0:T(8,128)(2,1)}, u32[]{:S(2)}, u32[]{:S(2)}) async-start(bf16[128,16,512]{2,1,0:T(8,128)(2,1)} %bitcast.34), calls=%async_computation | async-start | bytes 4194304 | tf_op jit(solution)/shard_map/all_to_all | solution.py:335
  49.3 29.1 %all-to-all-done = bf16[128,16,512]{2,1,0:T(8,128)(2,1)} async-done(((bf16[128,16,512]{2,1,0:T(8,128)(2,1)}), bf16[128,16,512]{2,1,0:T(8,128)(2,1)}, u32[]{:S(2)}, u32[]{:S(2)}) %all-to-all-start) | async-done | bytes 2097184 | tf_op jit(solution)/shard_map/all_to_all | solution.py:335
  78.4 8.2 %edge.1 = (bf16[2048,512]{1,0:T(8,128)(2,1)}, bf16[2048,512]{1,0:T(8,128)(2,1)}, bf16[2048,512]{1,0:T(8,128)(2,1)}) custom-call(bf16[2048,512]{1,0:T(8,128)(2,1)} %bitcast.5.rows_ref, bf16[512,512]{1,0:T(8,128)(2,1)S(1)} %copy-done.1, s32[2048,1]{1,0:T(8,128)S(1)} %reshape_reshape.4.dst_ref, bf16[320,512]{1,0:T(8,128)(2,1)S(1)} %convolution_convert_fusion.1.agg_ref), custom_call_target="tpu_custom_call" | custom-call | tf_op jit(solution)/shard_map/edge/pallas_call | solution.py:358
  86.6 4.4 %all-to-all-start.1 = ((bf16[128,16,512]{2,1,0:T(8,128)(2,1)}), bf16[128,16,512]{2,1,0:T(8,128)(2,1)S(1)}, u32[]{:S(2)}, u32[]{:S(2)}) async-start(bf16[128,16,512]{2,1,0:T(8,128)(2,1)} %bitcast.33), calls=%async_computation.1 | async-start | bytes 4194304 | tf_op jit(solution)/shard_map/all_to_all | solution.py:373
  91.3 9.8 %flip.1.patches_ref = bf16[9,512,1024]{2,1,0:T(8,128)(2,1)} custom-call(bf16[3,32,32,512]{3,2,1,0:T(8,128)(2,1)} %get-tuple-element.20.even_ref, bf16[3,33,32,512]{3,2,1,0:T(8,128)(2,1)} %get-tuple-element.21.odd_ref), custom_call_target="tpu_custom_call" | custom-call | bytes 16777216 | tf_op jit(solution)/shard_map/flip/pallas_call | solution.py:340
  102.7 2.9 %convolution_bitcast_fusion.1 = f32[1,512,512]{2,1,0:T(8,128)S(1)} fusion(bf16[2048,512]{1,0:T(8,128)(2,1)} %bitcast.5.rows_ref, bf16[2048,512]{1,0:T(8,128)(2,1)S(1)} %copy-done.10), kind=kOutput, calls=%fused_computation.5 | convolution fusion | flops 1073741824 | bytes 5242880 | tf_op jit(solution)/shard_map/dot_general | solution.py:21
  105.6 1.5 pad_maximum_fusion.small_ref
  107.1 14.6 %all-to-all-done.1 = bf16[128,16,512]{2,1,0:T(8,128)(2,1)S(1)} async-done(((bf16[128,16,512]{2,1,0:T(8,128)(2,1)}), bf16[128,16,512]{2,1,0:T(8,128)(2,1)S(1)}, u32[]{:S(2)}, u32[]{:S(2)}) %all-to-all-start.1) | async-done | bytes 2097184 | tf_op jit(solution)/shard_map/all_to_all | solution.py:373
  121.7 1.3 copy-done.4
  123.0 15.6 %sent_half.1 = (bf16[11,512,256]{2,1,0:T(8,128)(2,1)}, bf16[1024,512]{1,0:T(8,128)(2,1)S(1)}) custom-call(s32[1]{0:T(128)} %bitcast.9.half_ref, bf16[9,512,1024]{2,1,0:T(8,128)(2,1)} %flip.1.patches_ref, f32[2,512,512]{2,1,0:T(8,128)} %pad_maximum_fusion.small_ref, bf16[2048,512]{1,0:T(8,128)(2,1)} %bitcast.32, ...), custom_call_target="tpu_custom_call" | custom-call | tf_op jit(solution)/shard_map/sent_half/pallas_call | solution.py:392
  139.5 12.1 %kept_half.1 = f32[11,512,256]{2,1,0:T(8,128)} custom-call(s32[1]{0:T(128)} %bitcast.6.half_ref.core_ref, bf16[9,512,1024]{2,1,0:T(8,128)(2,1)} %flip.1.patches_ref, f32[2,512,512]{2,1,0:T(8,128)} %pad_maximum_fusion.small_ref, bf16[1024,512]{1,0:T(8,128)(2,1)S(1)} %get-tuple-element.25.stemout_ref), custom_call_target="tpu_custom_call" | custom-call | flops 2415919104 | bytes 20971520 | tf_op jit(solution)/shard_map/kept_half/pallas_call | solution.py:410
  151.7 3.3 %add_convert_fusion = bf16[11,512,256]{2,1,0:T(8,128)(2,1)S(1)} fusion(f32[11,512,256]{2,1,0:T(8,128)} %kept_half.1, bf16[11,512,256]{2,1,0:T(8,128)(2,1)S(1)} %collective-permute-done.3), kind=kLoop, calls=%fused_computation | loop fusion | flops 4325376 | bytes 11534336 | tf_op jit(solution)/shard_map/convert_element_type | solution.py:428
  155.0 42.8 %all_to_all.20 = bf16[64,88,256]{2,1,0:T(8,128)(2,1)S(1)} all-to-all(bf16[64,88,256]{2,1,0:T(8,128)(2,1)S(1)} %bitcast.31), channel_id=1, replica_groups=mesh['band'=16,'chip'=4,'core'=2] {'band','chip'}, dimensions={0} | all-to-all | bytes 5767168 | tf_op jit(solution)/shard_map/all_to_all | solution.py:430
  198.4 41.9 %all_to_all.21 = bf16[64,88,256]{2,1,0:T(8,128)(2,1)S(1)} all-to-all(bf16[64,88,256]{2,1,0:T(8,128)(2,1)S(1)} %broadcast_in_dim.36), channel_id=1, replica_groups=mesh['band'=16,'chip'=4,'core'=2] {'band','chip'}, dimensions={0} | all-to-all | bytes 5767168 | tf_op jit(solution)/shard_map/all_to_all | solution.py:435
  240.3 2.7 %collective-permute-start.4 = (bf16[11,512,256]{2,1,0:T(8,128)(2,1)S(1)}, bf16[11,512,256]{2,1,0:T(8,128)(2,1)S(1)}, u32[]{:S(2)}, u32[]{:S(2)}) collective-permute-start(bf16[11,512,256]{2,1,0:T(8,128)(2,1)S(1)} %bitcast.29), channel_id=1, source_target_pairs={{0,1},{1,0},{2,3},{3,2},{4,5},{5,4},{6,7},{7,6},{8,9},{9,8},{10,11... | collective-permute-start | bytes 8650760 | tf_op jit(solution)/shard_map/ppermute | solution.py:33
  243.0 1.1 convolution_convert_fusion
  244.0 3.8 %collective-permute-done.4.other_ref = bf16[11,512,256]{2,1,0:T(8,128)(2,1)S(1)} collective-permute-done((bf16[11,512,256]{2,1,0:T(8,128)(2,1)S(1)}, bf16[11,512,256]{2,1,0:T(8,128)(2,1)S(1)}, u32[]{:S(2)}, u32[]{:S(2)}) %collective-permute-start.4) | collective-permute-done | bytes 2883616 | tf_op jit(solution)/shard_map/ppermute | solution.py:33
  247.9 1.6 copy-done.5
  249.5 11.0 %final.1 = (f32[9,474,512]{2,1,0:T(8,128)}, f32[1,512]{1,0:T(1,128)}, f32[512,512]{1,0:T(8,128)}, f32[512,512]{1,0:T(8,128)}) custom-call(s32[1]{0:T(128)} %bitcast.6.half_ref.core_ref, bf16[11,512,256]{2,1,0:T(8,128)(2,1)} %bitcast.30, bf16[11,512,256]{2,1,0:T(8,128)(2,1)} %copy-done.5), custom_call_target="tpu_custom_call" | custom-call | tf_op jit(solution)/shard_map/final/pallas_call | solution.py:439
  (52 shorter events, 9.8 us)
Async XLA Ops:
  0.6 48.3 %copy-start = (bf16[512,512]{1,0:T(8,128)(2,1)S(1)}, bf16[512,512]{1,0:T(8,128)(2,1)}, u32[]{:S(2)}) copy-start(bf16[512,512]{1,0:T(8,128)(2,1)} %param.13) | copy-start | bytes 1572868
  1.4 20.1 %collective-permute-start.2 = (bf16[1,1,474]{2,1,0:T(2,128)(2,1)S(1)}, bf16[1,1,474]{2,1,0:T(2,128)(2,1)S(1)}, u32[]{:S(2)}, u32[]{:S(2)}) collective-permute-start(bf16[1,1,474]{2,1,0:T(2,128)(2,1)S(1)} %slice.11), channel_id=1, source_target_pairs={{0,9},{1,10},{2,11},{3,12},{4,13},{5,14},{6,15},{7,8},{8,17},{9,18... | collective-permute-start | bytes 2852 | tf_op jit(solution)/shard_map/ppermute | solution.py:285
  8.1 13.4 %collective-permute-start.1 = (bf16[1,64,474]{2,1,0:T(8,128)(2,1)S(1)}, bf16[1,64,474]{2,1,0:T(8,128)(2,1)S(1)}, u32[]{:S(2)}, u32[]{:S(2)}) collective-permute-start(bf16[1,64,474]{2,1,0:T(8,128)(2,1)S(1)} %slice.10), channel_id=1, source_target_pairs={{0,8},{8,16},{16,24},{24,32},{32,40},{40,48},{48,56},{56,64},{64,7... | collective-permute-start | bytes 182024 | tf_op jit(solution)/shard_map/ppermute | solution.py:284
  12.8 8.7 %collective-permute-start = (bf16[64,1,474]{2,1,0:T(2,128)(2,1)S(1)}, bf16[64,1,474]{2,1,0:T(2,128)(2,1)S(1)}, u32[]{:S(2)}, u32[]{:S(2)}) collective-permute-start(bf16[64,1,474]{2,1,0:T(2,128)(2,1)S(1)} %slice.9), channel_id=1, source_target_pairs={{0,1},{1,2},{2,3},{3,4},{4,5},{5,6},{6,7},{7,0},{8,9},{9,10},{10,1... | collective-permute-start | bytes 182024 | tf_op jit(solution)/shard_map/ppermute | solution.py:281
  16.7 4.9 %copy-start.2 = (f32[512]{0:T(512)S(1)}, f32[512]{0:T(512)}, u32[]{:S(2)}) copy-start(f32[512]{0:T(512)} %param.11) | copy-start | bytes 6148
  39.7 8.5 %copy-start.9 = (s32[1,128,16]{1,2,0:T(8,128)S(1)}, s32[1,128,16]{1,2,0:T(8,128)}, u32[]{:S(2)}) copy-start(s32[1,128,16]{1,2,0:T(8,128)} %param.15) | copy-start | bytes 24580
  39.7 9.2 %copy-start.6 = (bf16[320,512]{1,0:T(8,128)(2,1)S(1)}, bf16[320,512]{1,0:T(8,128)(2,1)}, u32[]{:S(2)}) copy-start(bf16[320,512]{1,0:T(8,128)(2,1)} %param.17) | copy-start | bytes 983044
  39.7 38.7 %copy-start.1 = (bf16[512,512]{1,0:T(8,128)(2,1)S(1)}, bf16[512,512]{1,0:T(8,128)(2,1)}, u32[]{:S(2)}) copy-start(bf16[512,512]{1,0:T(8,128)(2,1)} %w_ref.1) | copy-start | bytes 1572868
  39.7 38.6 %all-to-all-start = ((bf16[128,16,512]{2,1,0:T(8,128)(2,1)}), bf16[128,16,512]{2,1,0:T(8,128)(2,1)}, u32[]{:S(2)}, u32[]{:S(2)}) async-start(bf16[128,16,512]{2,1,0:T(8,128)(2,1)} %bitcast.34), calls=%async_computation | async-start | bytes 4194304 | tf_op jit(solution)/shard_map/all_to_all | solution.py:335
  86.6 35.0 %all-to-all-start.1 = ((bf16[128,16,512]{2,1,0:T(8,128)(2,1)}), bf16[128,16,512]{2,1,0:T(8,128)(2,1)S(1)}, u32[]{:S(2)}, u32[]{:S(2)}) async-start(bf16[128,16,512]{2,1,0:T(8,128)(2,1)} %bitcast.33), calls=%async_computation.1 | async-start | bytes 4194304 | tf_op jit(solution)/shard_map/all_to_all | solution.py:373
  91.3 9.8 %copy-start.11 = (bf16[2048,512]{1,0:T(8,128)(2,1)S(1)}, bf16[2048,512]{1,0:T(8,128)(2,1)}, u32[]{:S(2)}) copy-start(bf16[2048,512]{1,0:T(8,128)(2,1)} %get-tuple-element.19) | copy-start | bytes 6291460
  101.1 1.6 copy-start.10
  102.0 0.7 copy-start.7
  121.7 1.3 copy-start.4
  138.6 13.1 %collective-permute-start.3 = (bf16[11,512,256]{2,1,0:T(8,128)(2,1)}, bf16[11,512,256]{2,1,0:T(8,128)(2,1)S(1)}, u32[]{:S(2)}, u32[]{:S(2)}) collective-permute-start(bf16[11,512,256]{2,1,0:T(8,128)(2,1)} %get-tuple-element.26), channel_id=1, source_target_pairs={{0,1},{1,0},{2,3},{3,2},{4,5},{5,4},{6,7},{7,6},{8,9},{9,8},{10,11... | collective-permute-start | bytes 8650760 | tf_op jit(solution)/shard_map/ppermute | solution.py:33
  198.3 44.6 %copy-start.8 = (bf16[320,512]{1,0:T(8,128)(2,1)S(1)}, bf16[320,512]{1,0:T(8,128)(2,1)}, u32[]{:S(2)}) copy-start(bf16[320,512]{1,0:T(8,128)(2,1)} %copy-done.7) | copy-start | bytes 983044
  240.3 7.6 %copy-start.3 = (bf16[64,88,256]{2,1,0:T(8,128)(2,1)}, bf16[64,88,256]{2,1,0:T(8,128)(2,1)S(1)}, u32[]{:S(2)}) copy-start(bf16[64,88,256]{2,1,0:T(8,128)(2,1)S(1)} %all_to_all.21) | copy-start | bytes 8650756
  240.3 7.6 %collective-permute-start.4 = (bf16[11,512,256]{2,1,0:T(8,128)(2,1)S(1)}, bf16[11,512,256]{2,1,0:T(8,128)(2,1)S(1)}, u32[]{:S(2)}, u32[]{:S(2)}) collective-permute-start(bf16[11,512,256]{2,1,0:T(8,128)(2,1)S(1)} %bitcast.29), channel_id=1, source_target_pairs={{0,1},{1,0},{2,3},{3,2},{4,5},{5,4},{6,7},{7,6},{8,9},{9,8},{10,11... | collective-permute-start | bytes 8650760 | tf_op jit(solution)/shard_map/ppermute | solution.py:33
  247.9 1.6 copy-start.5

commit v2 on v1

v2 whole, which is shorter than its diff:
```python
import functools

import jax
import jax.numpy as jnp
from jax import lax
from jax.experimental import pallas as pl
from jax.experimental.pallas import tpu as pltpu
from jax.sharding import Mesh, PartitionSpec as P

CHIPS = ("band", "chip")
EVERY = ("band", "chip", "core")
TAPS = 9
MIB = 1024 * 1024
TILE = 256


def f32_dot(first, second):
    return jnp.dot(first, second, preferred_element_type=jnp.float32)


def inner_dot(first, second):
    return lax.dot_general(
        first, second, (((0,), (0,)), ((), ())), preferred_element_type=jnp.float32
    )


def right_dot(first, second):
    return lax.dot_general(
        first, second, (((1,), (1,)), ((), ())), preferred_element_type=jnp.float32
    )


def core_swap(array):
    return lax.ppermute(array, "core", [(0, 1), (1, 0)])


def whole(memory=pltpu.VMEM):
    return pl.BlockSpec(memory_space=memory)


def params(mib):
    return pltpu.CompilerParams(vmem_limit_bytes=mib * MIB)


def cost(flops, moved):
    return pl.CostEstimate(flops=int(flops), bytes_accessed=int(moved), transcendentals=0)


def rows_at(number, size=TILE):
    return pl.ds(number * size, size)


def column_picker(image_rows, cols, parts):
    half = cols // 2
    shape = (3 * image_rows * half, image_rows * cols)
    out = lax.broadcasted_iota(jnp.int32, shape, 0)
    inside = lax.broadcasted_iota(jnp.int32, shape, 1)
    per_tap = image_rows * half
    tap = out // per_tap
    rest = out - tap * per_tap
    line = rest // half
    col = 2 * (rest - line * half) + tap - 1
    if parts == 2:
        pairs = image_rows // 2
        parity = line // pairs
        line = 2 * (line - parity * pairs) + parity
    hit = (col >= 0) & (inside == line * cols + col)
    return jnp.where(hit, 1.0, 0.0).astype(jnp.bfloat16)


def stem_kernel(
    west_ref, north_ref, corner_ref, picker_ref, north_picker_ref, bias_ref, source_ref,
    grid_hbm, w_hbm, even_hbm, odd_hbm, slope_hbm, out_hbm,
    grid, raw, weights, even, odd, latent, slope, out, in_sems, w_sems, out_sems, slope_sems, row_sems,
):
    rows, cols, channels = grid.shape
    half_rows, half_cols = rows // 2, cols // 2
    width = even.shape[-1]
    chunks = in_sems.shape[0]
    per_chunk = rows // chunks
    bf16 = jnp.bfloat16

    loads = [
        pltpu.make_async_copy(
            grid_hbm.at[rows_at(chunk, per_chunk)], grid.at[rows_at(chunk, per_chunk)], in_sems.at[chunk]
        )
        for chunk in range(chunks)
    ]
    w_loads = [
        pltpu.make_async_copy(w_hbm.at[tap], raw.at[tap], w_sems.at[tap]) for tap in range(TAPS)
    ]
    for copy in loads + w_loads:
        copy.start()

    tail = width - 128
    even[:, :, :, tail:] = jnp.zeros((3, half_rows, half_cols, 128), bf16)
    odd[:, :, :, tail:] = jnp.zeros((3, half_rows + 1, half_cols, 128), bf16)
    gap = channels // 16 * 16
    for tap in range(TAPS):
        weights[tap * width + gap : (tap + 1) * width] = jnp.zeros((width - gap, width), bf16)
    picker = picker_ref[...]
    north = f32_dot(north_picker_ref[...], north_ref[0]).astype(bf16)
    for tap in range(3):
        odd[tap, 0, :, :channels] = north[tap * half_cols : (tap + 1) * half_cols]

    for chunk in range(chunks):
        loads[chunk].wait()
        for group in range(chunk * per_chunk // 4, (chunk + 1) * per_chunk // 4):
            block = grid[4 * group : 4 * group + 4].reshape(4 * cols, channels)
            picked = f32_dot(picker, block).astype(bf16).reshape(3, 2, 2, half_cols, channels)
            for tap in range(3):
                even[tap, 2 * group : 2 * group + 2, :, :channels] = picked[tap, 0]
                odd[tap, 2 * group + 1 : 2 * group + 3, :, :channels] = picked[tap, 1]

    def patch(target, first, count, column):
        old = target[0, first : first + count, 0:16, :channels].astype(jnp.float32)
        line = lax.broadcasted_iota(jnp.int32, old.shape, 1)
        new = jnp.where(line == 0, column.astype(jnp.float32), old)
        target[0, first : first + count, 0:16, :channels] = new.astype(bf16)

    patch(even, 0, half_rows, west_ref[:, 0])
    patch(odd, 1, half_rows, west_ref[:, 1])
    patch(odd, 0, 1, corner_ref[...])
    phase_copies = [
        pltpu.make_async_copy(even, even_hbm, out_sems.at[0]),
        pltpu.make_async_copy(odd, odd_hbm, out_sems.at[1]),
    ]
    for tap in range(TAPS):
        w_loads[tap].wait()
        weights[tap * width : tap * width + channels] = raw[tap]
    for copy in phase_copies:
        copy.start()

    tile_rows = TILE // half_cols
    slope_copies = []
    for step in range(half_rows // tile_rows):
        pieces = []
        for row_tap in range(3):
            for col_tap in range(3):
                first = step * tile_rows + (row_tap // 2)
                held = even if row_tap == 1 else odd
                pieces.append(held[col_tap, first : first + tile_rows].reshape(TILE, width))
        pre = f32_dot(jnp.concatenate(pieces, axis=1), weights[...]) + bias_ref[...]
        sigmoid = jax.nn.sigmoid(pre)
        here = rows_at(step)
        slope[here] = sigmoid * (1.0 + pre * (1.0 - sigmoid))
        latent[here] = (pre * sigmoid).astype(bf16)
        copy = pltpu.make_async_copy(slope.at[here], slope_hbm.at[here], slope_sems.at[step])
        copy.start()
        slope_copies.append(copy)

    points = latent.shape[0]
    row_copies = []
    for step in range(out.shape[0] // TILE):
        here = rows_at(step)
        point = lax.broadcasted_iota(jnp.int32, (TILE, points), 1)
        pick = jnp.where(point == source_ref[here], 1.0, 0.0).astype(bf16)
        out[here] = f32_dot(pick, latent[...]).astype(bf16)
        copy = pltpu.make_async_copy(out.at[here], out_hbm.at[here], row_sems.at[step])
        copy.start()
        row_copies.append(copy)

    for copy in phase_copies + slope_copies + row_copies:
        copy.wait()


def flip_kernel(channels, even_ref, odd_ref, out_ref):
    number = pl.program_id(0)
    row_tap = number // 3
    col_tap = number % 3
    half_rows, half_cols, width = even_ref.shape[1:]

    def write(values):
        flipped = values.reshape(half_rows * half_cols, width).T
        line = lax.broadcasted_iota(jnp.int32, flipped.shape, 0)
        ones = (line == channels) & (number == 0)
        out_ref[0] = jnp.where(ones, 1.0, flipped.astype(jnp.float32)).astype(jnp.bfloat16)

    @pl.when(row_tap == 1)
    def _():
        write(even_ref[col_tap])

    @pl.when(row_tap != 1)
    def _():
        write(odd_ref[col_tap, pl.ds(row_tap // 2, half_rows)])


def edge_kernel(
    w_ref, dst_ref, agg_ref, rows_hbm, back_hbm, message_hbm, grad_hbm,
    rows, back, message, grad, in_sems, back_sems, message_sems, grad_sems,
):
    nodes = agg_ref.shape[0]
    tiles = rows.shape[0] // TILE
    bf16 = jnp.bfloat16
    loads = [
        pltpu.make_async_copy(rows_hbm.at[rows_at(step)], rows.at[rows_at(step)], in_sems.at[step])
        for step in range(tiles)
    ]
    for copy in loads:
        copy.start()
    copies = []
    weights = w_ref[...]
    for step in range(tiles):
        here = rows_at(step)
        node = lax.broadcasted_iota(jnp.int32, (TILE, nodes), 1)
        pick = jnp.where(node == dst_ref[here], 1.0, 0.0).astype(bf16)
        grad_msg = f32_dot(pick, agg_ref[...])
        loads[step].wait()
        pre = f32_dot(rows[here], weights)
        sigmoid = jax.nn.sigmoid(pre)
        message[here] = (pre * sigmoid).astype(bf16)
        grad_pre = (grad_msg * (sigmoid * (1.0 + pre * (1.0 - sigmoid)))).astype(bf16)
        grad[here] = grad_pre
        back[here] = right_dot(grad_pre, weights).astype(bf16)
        for kept, placed, sems in (
            (back, back_hbm, back_sems), (message, message_hbm, message_sems), (grad, grad_hbm, grad_sems),
        ):
            copy = pltpu.make_async_copy(kept.at[here], placed.at[here], sems.at[step])
            copy.start()
            copies.append(copy)
    for copy in copies:
        copy.wait()


def tap_products(columns, stemout_ref, smalls, patches_hbm, out_hbm, patches, out, in_sems, out_sems, ready):
    loads = [
        pltpu.make_async_copy(patches_hbm.at[tap], patches.at[tap], in_sems.at[tap])
        for tap in range(TAPS)
    ]
    for copy in loads:
        copy.start()
    ready()
    copies = [
        pltpu.make_async_copy(out.at[number], out_hbm.at[number], out_sems.at[number])
        for number in range(TAPS + 2)
    ]
    for number, small in enumerate(smalls):
        out[TAPS + number] = small[:, columns].astype(out.dtype)
        copies[TAPS + number].start()
    for tap in range(TAPS):
        loads[tap].wait()
        out[tap] = f32_dot(patches[tap], stemout_ref[:, columns]).astype(out.dtype)
        copies[tap].start()
    for copy in copies:
        copy.wait()


def half_columns(half, half_width):
    return pl.ds(pl.multiple_of(half * half_width, half_width), half_width)


def sent_kernel(
    half_ref, edge_ref, node_ref, returned_ref, source_ref, slope_ref, patches_hbm,
    out_hbm, stemout_ref, patches, out, in_sems, out_sems,
):
    points = stemout_ref.shape[0]
    slots = returned_ref.shape[0]

    def ready():
        for step in range(points // TILE):
            here = rows_at(step)
            point = lax.broadcasted_iota(jnp.int32, (TILE, slots), 0) + step * TILE
            pick = jnp.where(point == source_ref[...], 1.0, 0.0).astype(jnp.bfloat16)
            grad_latent = f32_dot(pick, returned_ref[...])
            stemout_ref[here] = (grad_latent * slope_ref[here]).astype(jnp.bfloat16)

    tap_products(
        half_columns(half_ref[0], out.shape[-1]), stemout_ref, (edge_ref, node_ref),
        patches_hbm, out_hbm, patches, out, in_sems, out_sems, ready,
    )


def kept_kernel(
    half_ref, edge_ref, node_ref, stemout_ref, patches_hbm, out_hbm, patches, out, in_sems, out_sems
):
    tap_products(
        half_columns(half_ref[0], out.shape[-1]), stemout_ref, (edge_ref, node_ref),
        patches_hbm, out_hbm, patches, out, in_sems, out_sems, lambda: None,
    )


def final_kernel(
    half_ref, sums_ref, *refs
):
    stem_hbm, bias_hbm, edge_hbm, node_hbm, stem, bias, square, stem_sems, sems = refs[-9:]
    channels = stem.shape[1]
    columns = half_columns(half_ref[0], stem.shape[-1])
    bias[...] = sums_ref[0, channels : channels + 1].astype(jnp.float32)
    copies = [pltpu.make_async_copy(bias, bias_hbm.at[:, columns], sems.at[0])]
    copies[0].start()
    for tap in range(TAPS):
        stem[tap] = sums_ref[tap, :channels].astype(jnp.float32)
        copies.append(
            pltpu.make_async_copy(stem.at[tap], stem_hbm.at[tap, :, columns], stem_sems.at[tap])
        )
        copies[-1].start()
    for number, placed in enumerate((edge_hbm, node_hbm)):
        square[number] = sums_ref[TAPS + number].astype(jnp.float32)
        copies.append(
            pltpu.make_async_copy(square.at[number], placed.at[:, columns], sems.at[1 + number])
        )
        copies[-1].start()
    for copy in copies:
        copy.wait()


def shards(
    grid_input, w_stem, b_stem, w_edge, w_node, src_index, dst_index, counts, mesh_cotangent
):
    rows_here, cols_here, channels = grid_input.shape
    width = w_edge.shape[0]
    bands = lax.axis_size("band")
    columns = lax.axis_size("chip") * 2
    chips = bands * lax.axis_size("chip")
    core = lax.axis_index("core")
    device_count = 2 * chips
    slot_count = src_index.shape[2]
    slots = device_count * slot_count
    half_rows = rows_here // 2
    half_cols = cols_here // 2
    points = half_rows * half_cols
    half_width = width // 2
    node_total = mesh_cotangent.shape[0]
    bf16, f32 = jnp.bfloat16, jnp.float32

    west = lax.ppermute(
        grid_input[:, -1:, :], ("chip", "core"), [(i, (i + 1) % columns) for i in range(columns)]
    )
    north = lax.ppermute(grid_input[-1:], "band", [(i, i + 1) for i in range(bands - 1)])
    corner = lax.ppermute(
        grid_input[-1:, -1:],
        EVERY,
        [
            (i * columns + j, (i + 1) * columns + (j + 1) % columns)
            for i in range(bands - 1)
            for j in range(columns)
        ],
    )
    flat_src = src_index.reshape(device_count, slot_count)
    slot_live = jnp.arange(slot_count, dtype=jnp.int32)[None, :] < counts.reshape(device_count, 1)
    source = jnp.where(slot_live, flat_src, -1)

    steps = slots // TILE
    even, odd, slope, outgoing = pl.pallas_call(
        stem_kernel,
        out_shape=(
            jax.ShapeDtypeStruct((3, half_rows, half_cols, width), bf16),
            jax.ShapeDtypeStruct((3, half_rows + 1, half_cols, width), bf16),
            jax.ShapeDtypeStruct((points, width), f32),
            jax.ShapeDtypeStruct((slots, width), bf16),
        ),
        in_specs=[whole()] * 7 + [whole(pl.ANY)] * 2,
        out_specs=(whole(pl.ANY),) * 4,
        scratch_shapes=[
            pltpu.VMEM((rows_here, cols_here, channels), bf16),
            pltpu.VMEM((TAPS, channels, width), bf16),
            pltpu.VMEM((TAPS * width, width), bf16),
            pltpu.VMEM((3, half_rows, half_cols, width), bf16),
            pltpu.VMEM((3, half_rows + 1, half_cols, width), bf16),
            pltpu.VMEM((points, width), bf16),
            pltpu.VMEM((points, width), f32),
            pltpu.VMEM((slots, width), bf16),
            pltpu.SemaphoreType.DMA((4,)),
            pltpu.SemaphoreType.DMA((TAPS,)),
            pltpu.SemaphoreType.DMA((2,)),
            pltpu.SemaphoreType.DMA((points // TILE,)),
            pltpu.SemaphoreType.DMA((steps,)),
        ],
        compiler_params=params(40),
        name="stem",
    )(
        west.reshape(half_rows, 2, 1, channels),
        north,
        corner,
        column_picker(4, cols_here, 2),
        column_picker(1, cols_here, 1),
        b_stem.reshape(1, width),
        source.reshape(slots, 1),
        grid_input,
        w_stem,
    )

    incoming = lax.all_to_all(
        outgoing.reshape(device_count, slot_count, width), EVERY, split_axis=0, concat_axis=0, tiled=True
    )
    arrived = incoming.reshape(slots, width)

    patches = pl.pallas_call(
        functools.partial(flip_kernel, channels),
        grid=(TAPS,),
        out_shape=jax.ShapeDtypeStruct((TAPS, width, points), bf16),
        in_specs=[
            pl.BlockSpec((3, half_rows, half_cols, width), lambda t: (0, 0, 0, 0)),
            pl.BlockSpec((3, half_rows + 1, half_cols, width), lambda t: (0, 0, 0, 0)),
        ],
        out_specs=pl.BlockSpec((1, width, points), lambda t: (t, 0, 0)),
        compiler_params=params(24),
        cost_estimate=cost(0, 16 * MIB),
        name="flip",
    )(even, odd)
    grad_agg = right_dot(mesh_cotangent, w_node).astype(bf16)
    dst_flat = dst_index.reshape(slots)

    back, messages, grad_pre = pl.pallas_call(
        edge_kernel,
        out_shape=(jax.ShapeDtypeStruct((slots, width), bf16),) * 3,
        in_specs=[whole()] * 3 + [whole(pl.ANY)],
        out_specs=(whole(pl.ANY),) * 3,
        scratch_shapes=[pltpu.VMEM((slots, width), bf16)] * 4
        + [pltpu.SemaphoreType.DMA((steps,))] * 4,
        compiler_params=params(24),
        name="edge",
    )(w_edge, dst_flat.reshape(slots, 1), grad_agg, arrived)

    returned = lax.all_to_all(
        back.reshape(device_count, slot_count, width), EVERY, split_axis=0, concat_axis=0, tiled=True
    ).reshape(slots, width)

    node_ids = jnp.arange(node_total, dtype=jnp.int32)
    onehot = (node_ids[:, None] == dst_flat[None, :]).astype(bf16)
    aggregate = f32_dot(onehot, messages).astype(bf16)
    mesh_out = f32_dot(aggregate, w_node).astype(bf16)
    grad_node = inner_dot(aggregate, mesh_cotangent)
    grad_edge = inner_dot(arrived, grad_pre)
    mesh_out, grad_edge, grad_node = lax.optimization_barrier((mesh_out, grad_edge, grad_node))

    blocks = TAPS + 2
    other_half = (1 - core).reshape(1)
    own_half = core.reshape(1)
    half_shape = jax.ShapeDtypeStruct((blocks, width, half_width), bf16)
    tap_scratch = [
        pltpu.VMEM((TAPS, width, points), bf16),
        pltpu.VMEM((blocks, width, half_width), bf16),
        pltpu.SemaphoreType.DMA((TAPS,)),
        pltpu.SemaphoreType.DMA((blocks,)),
    ]
    product_flops = 2 * TAPS * width * points * half_width
    sent, stemout = pl.pallas_call(
        sent_kernel,
        out_shape=(half_shape, jax.ShapeDtypeStruct((points, width), bf16)),
        in_specs=[whole(pltpu.SMEM)] + [whole()] * 5 + [whole(pl.ANY)],
        out_specs=(whole(pl.ANY), whole()),
        scratch_shapes=tap_scratch,
        compiler_params=params(32),
        name="sent_half",
    )(other_half, grad_edge, grad_node, returned, source.reshape(1, slots), slope, patches)
    received = core_swap(sent)
    kept = pl.pallas_call(
        kept_kernel,
        out_shape=half_shape,
        in_specs=[whole(pltpu.SMEM)] + [whole()] * 3 + [whole(pl.ANY)],
        out_specs=whole(pl.ANY),
        scratch_shapes=tap_scratch,
        compiler_params=params(28),
        cost_estimate=cost(product_flops, 14 * MIB),
        name="kept_half",
    )(own_half, grad_edge, grad_node, stemout, patches)

    chip_sum = (kept.astype(f32) + received.astype(f32)).astype(bf16)
    chunk = blocks * width // chips
    pieces = lax.all_to_all(
        chip_sum.reshape(chips, chunk, half_width), CHIPS, split_axis=0, concat_axis=0, tiled=True
    )
    summed = jnp.sum(pieces.astype(f32), axis=0).astype(bf16)
    spread = jnp.broadcast_to(summed[None], (chips, chunk, half_width))
    gathered = lax.all_to_all(spread, CHIPS, split_axis=0, concat_axis=0, tiled=True)
    mine = gathered.reshape(blocks, width, half_width)
    other = core_swap(mine)

    out_shape = (
        jax.ShapeDtypeStruct((TAPS, channels, width), f32),
        jax.ShapeDtypeStruct((1, width), f32),
        jax.ShapeDtypeStruct((width, width), f32),
        jax.ShapeDtypeStruct((width, width), f32),
    )

    def final(half, sums, before, name):
        return pl.pallas_call(
            final_kernel,
            out_shape=out_shape,
            in_specs=[whole(pltpu.SMEM), whole()] + [whole(pl.ANY)] * len(before),
            out_specs=(whole(pl.ANY),) * 4,
            scratch_shapes=[
                pltpu.VMEM((TAPS, channels, half_width), f32),
                pltpu.VMEM((1, half_width), f32),
                pltpu.VMEM((2, width, half_width), f32),
                pltpu.SemaphoreType.DMA((TAPS,)),
                pltpu.SemaphoreType.DMA((3,)),
            ],
            input_output_aliases={2 + i: i for i in range(len(before))},
            compiler_params=params(20),
            cost_estimate=cost(0, 9 * MIB),
            name=name,
        )(half, sums, *before)

    first_half = final(own_half, mine, (), "final_mine")
    grad_stem, grad_bias, out_edge, out_node = final(other_half, other, first_half, "final_other")
    return (mesh_out, grad_stem, grad_bias.reshape(width), out_edge, out_node)


def solution(mesh):
    bands, columns = mesh.devices.shape
    fine = Mesh(mesh.devices.reshape(bands, columns // 2, 2), EVERY)
    in_specs = (
        P("band", ("chip", "core"), None),
        P(),
        P(),
        P(),
        P(),
        P(EVERY, None, None),
        P(EVERY, None, None),
        P(EVERY, None),
        P(EVERY, None),
    )
    out_specs = (P(EVERY, None), P(), P(), P(), P())
    return jax.shard_map(shards, mesh=fine, in_specs=in_specs, out_specs=out_specs, check_vma=False)
```

time: 262 us -> 249 us (0.950)
  Pallas kernels: 74.9 us -> 51.1 us
  local copies, waits for them, and re-layouts: 14 us -> 32.3 us
  other arithmetic: 6.7 us -> 2.8 us
  waiting for transfers between devices: 47.5 us -> 44.7 us
    unnamed x26 -> x58, local copies, waits for them, and re-layouts: 4.12 us -> 26.3 us
    pallas_call x4 -> x5, Pallas kernels: 47 us -> 31.7 us  [the longest x1 11.1 us: shards(): pl.pallas_call(sent_kernel, out_shape=(half_shape, jax.ShapeDtypeStruct((...]
    pallas_call x1, Pallas kernels: 9.78 us -> 3.32 us  [shards(): pl.pallas_call(functools.partial(flip_kernel, channels), grid=(TAPS,), ou...]
    pad x1 -> x0, local copies, waits for them, and re-layouts: 4.84 us -> none  [shards(): jnp.pad(w_stem, ((0, 0), (0, width - channels), (0, 0)))]
  transfers between devices with their start and end apart: 7 -> 7, of which waited for: 3 -> 3; matrix products, arithmetic and copies ran while one was open for 7% -> 5% of each run, Pallas kernels for 8% -> 5%
where the time goes in v2:
time: 249 us; the launch traced here: 248 us
  blocking collectives  84.4 us (34%)
  Pallas kernels  51.1 us (21%)
  waiting for transfers between devices  44.7 us (18%)
  local copies, waits for them, and re-layouts  32.3 us (13%)
  starting transfers between devices  27 us (11%)
  matrix products  4.96 us (2%)
  other arithmetic  2.8 us (1%)
    all_to_all x1, blocking collectives, shards(): lax.all_to_all(chip_sum.reshape(chips, chunk, half_width), CHIPS, split_a...  42.6 us
    all_to_all x1, blocking collectives, shards(): lax.all_to_all(spread, CHIPS, split_axis=0, concat_axis=0, tiled=True)  41.8 us
    all_to_all x1, waiting for transfers between devices, shards(): lax.all_to_all(outgoing.reshape(device_count, slot_count, width), EVERY,...  26.9 us
    unnamed x58, local copies, waits for them, and re-layouts  26.3 us
    pallas_call x1, Pallas kernels, shards(): pl.pallas_call(stem_kernel, out_shape=(jax.ShapeDtypeStruct((3, half_rows...  16.1 us
    all_to_all x1, waiting for transfers between devices, shards(): lax.all_to_all(back.reshape(device_count, slot_count, width), EVERY, spli...  15.5 us
    pallas_call x1, Pallas kernels, shards(): pl.pallas_call(sent_kernel, out_shape=(half_shape, jax.ShapeDtypeStruct((...  11.1 us
    pallas_call x1, Pallas kernels, shards(): pl.pallas_call(edge_kernel, out_shape=(jax.ShapeDtypeStruct((slots, width...  8.42 us
  transfers between devices with their start and end apart: 7, of which 3 were waited for; matrix products, arithmetic and copies ran while one was open for 5% of the time, Pallas kernels for 5%

profile of v2, /device:TPU:1, one launch (start us, length us, event | category | flops | bytes accessed | tf_op | source)
XLA Modules:
  0.0 248.4 jit_solution(17699880754860847425)
XLA Ops:
  1.4 5.8 %collective-permute-start.2 = (bf16[1,1,474]{2,1,0:T(2,128)(2,1)S(1)}, bf16[1,1,474]{2,1,0:T(2,128)(2,1)S(1)}, u32[]{:S(2)}, u32[]{:S(2)}) collective-permute-start(bf16[1,1,474]{2,1,0:T(2,128)(2,1)S(1)} %slice.11), channel_id=1, source_target_pairs={{0,9},{1,10},{2,11},{3,12},{4,13},{5,14},{6,15},{7,8},{8,17},{9,18... | collective-permute-start | bytes 2852 | tf_op jit(solution)/shard_map/ppermute | solution.py:330
  8.1 3.5 %collective-permute-start.1 = (bf16[1,64,474]{2,1,0:T(8,128)(2,1)S(1)}, bf16[1,64,474]{2,1,0:T(8,128)(2,1)S(1)}, u32[]{:S(2)}, u32[]{:S(2)}) collective-permute-start(bf16[1,64,474]{2,1,0:T(8,128)(2,1)S(1)} %slice.10), channel_id=1, source_target_pairs={{0,8},{8,16},{16,24},{24,32},{32,40},{40,48},{48,56},{56,64},{64,7... | collective-permute-start | bytes 182024 | tf_op jit(solution)/shard_map/ppermute | solution.py:329
  16.7 16.1 %stem.1 = (bf16[3,32,32,512]{3,2,1,0:T(8,128)(2,1)S(1)}, bf16[3,33,32,512]{3,2,1,0:T(8,128)(2,1)S(1)}, f32[1024,512]{1,0:T(8,128)S(1)}, bf16[2048,512]{1,0:T(8,128)(2,1)S(1)}) custom-call(bf16[32,2,1,474]{3,2,1,0:T(2,128)(2,1)S(1)} %bitcast.29, bf16[1,64,474]{2,1,0:T(8,128)(2,1)S(1)} %collective-permute-done.1.north_ref, ...), custom_call_target="tpu_custom_call" | custom-call | tf_op jit(solution)/shard_map/stem/pallas_call | solution.py:344
  32.8 1.7 copy-done.7
  34.5 1.6 copy-done.9
  38.8 8.0 %all-to-all-start = ((bf16[128,16,512]{2,1,0:T(8,128)(2,1)}), bf16[128,16,512]{2,1,0:T(8,128)(2,1)S(1)}, u32[]{:S(2)}, u32[]{:S(2)}) async-start(bf16[128,16,512]{2,1,0:T(8,128)(2,1)} %bitcast.28), calls=%async_computation | async-start | bytes 4194304 | tf_op jit(solution)/shard_map/all_to_all | solution.py:383
  50.4 26.9 %all-to-all-done = bf16[128,16,512]{2,1,0:T(8,128)(2,1)S(1)} async-done(((bf16[128,16,512]{2,1,0:T(8,128)(2,1)}), bf16[128,16,512]{2,1,0:T(8,128)(2,1)S(1)}, u32[]{:S(2)}, u32[]{:S(2)}) %all-to-all-start) | async-done | bytes 2097184 | tf_op jit(solution)/shard_map/all_to_all | solution.py:383
  77.3 2.0 copy-done.6
  79.3 8.4 %edge.1 = (bf16[2048,512]{1,0:T(8,128)(2,1)S(1)}, bf16[2048,512]{1,0:T(8,128)(2,1)S(1)}, bf16[2048,512]{1,0:T(8,128)(2,1)S(1)}) custom-call(bf16[512,512]{1,0:T(8,128)(2,1)S(1)} %copy-done.15, s32[2048,1]{1,0:T(8,128)S(1)} %copy-done.6, bf16[320,512]{1,0:T(8,128)(2,1)S(1)} %convolution_convert_fusion.1.agg_ref, bf16[2048,512]{1,0:T(8,128)(2,1)S(1)} %bitcast.25), custom_call_target="tpu_custom_call" | custom-call | tf_op jit(solution)/shard_map/edge/pallas_call | solution.py:404
  91.7 5.4 %all-to-all-start.1 = ((bf16[128,16,512]{2,1,0:T(8,128)(2,1)}), bf16[128,16,512]{2,1,0:T(8,128)(2,1)}, u32[]{:S(2)}, u32[]{:S(2)}) async-start(bf16[128,16,512]{2,1,0:T(8,128)(2,1)} %bitcast.27), calls=%async_computation.1 | async-start | bytes 4194304 | tf_op jit(solution)/shard_map/all_to_all | solution.py:415
  97.5 1.9 copy-done.8
  99.4 1.9 copy-done.10
  101.3 3.3 %flip.1.patches_hbm = bf16[9,512,1024]{2,1,0:T(8,128)(2,1)S(1)} custom-call(bf16[3,32,32,512]{3,2,1,0:T(8,128)(2,1)S(1)} %copy-done.10, bf16[3,33,32,512]{3,2,1,0:T(8,128)(2,1)S(1)} %copy-done.8), custom_call_target="tpu_custom_call" | custom-call | bytes 16777216 | tf_op jit(solution)/shard_map/flip/pallas_call | solution.py:388
  104.6 3.6 %copy-done.2 = bf16[9,512,1024]{2,1,0:T(8,128)(2,1)} copy-done((bf16[9,512,1024]{2,1,0:T(8,128)(2,1)}, bf16[9,512,1024]{2,1,0:T(8,128)(2,1)S(1)}, u32[]{:S(2)}) %copy-start.2) | copy-done | bytes 9437208
  112.0 15.5 %all-to-all-done.1 = bf16[128,16,512]{2,1,0:T(8,128)(2,1)} async-done(((bf16[128,16,512]{2,1,0:T(8,128)(2,1)}), bf16[128,16,512]{2,1,0:T(8,128)(2,1)}, u32[]{:S(2)}, u32[]{:S(2)}) %all-to-all-start.1) | async-done | bytes 2097184 | tf_op jit(solution)/shard_map/all_to_all | solution.py:415
  127.5 3.7 %copy-done.3 = bf16[9,512,1024]{2,1,0:T(8,128)(2,1)S(1)} copy-done((bf16[9,512,1024]{2,1,0:T(8,128)(2,1)S(1)}, bf16[9,512,1024]{2,1,0:T(8,128)(2,1)}, u32[]{:S(2)}) %copy-start.3) | copy-done | bytes 9437208
  132.8 11.1 %sent_half.1 = (bf16[11,512,256]{2,1,0:T(8,128)(2,1)S(1)}, bf16[1024,512]{1,0:T(8,128)(2,1)S(1)}) custom-call(s32[1]{0:T(128)} %bitcast.5.half_ref, f32[512,512]{1,0:T(8,128)S(1)} %fusion.19.edge_ref, f32[512,512]{1,0:T(8,128)S(1)} %fusion.20.node_ref, bf16[2048,512]{1,0:T(8,128)(2,1)} %bitcast.8.returned_ref, ...), custom_call_target="tpu_custom_call" | custom-call | tf_op jit(solution)/shard_map/sent_half/pallas_call | solution.py:438
  145.1 7.1 %kept_half.1 = bf16[11,512,256]{2,1,0:T(8,128)(2,1)S(1)} custom-call(s32[1]{0:T(128)} %bitcast.6.half_ref, f32[512,512]{1,0:T(8,128)S(1)} %fusion.19.edge_ref, f32[512,512]{1,0:T(8,128)S(1)} %fusion.20.node_ref, bf16[1024,512]{1,0:T(8,128)(2,1)S(1)} %get-tuple-element.35.stemout_ref, bf16[9,512,1024]{2,1,0:T(8,128)(2,1)S(1)} %bitcast.22), custom_call_target="tpu_custom_call" | custom-call | flops 2415919104 | bytes 14680064 | tf_op jit(solution)/shard_map/kept_half/pallas_call | solution.py:448
  153.1 42.6 %all_to_all.20 = bf16[64,88,256]{2,1,0:T(8,128)(2,1)S(1)} all-to-all(bf16[64,88,256]{2,1,0:T(8,128)(2,1)S(1)} %bitcast.31), channel_id=1, replica_groups=mesh['band'=16,'chip'=4,'core'=2] {'band','chip'}, dimensions={0} | all-to-all | bytes 5767168 | tf_op jit(solution)/shard_map/all_to_all | solution.py:461
  196.3 41.8 %all_to_all.21 = bf16[64,88,256]{2,1,0:T(8,128)(2,1)S(1)} all-to-all(bf16[64,88,256]{2,1,0:T(8,128)(2,1)S(1)} %broadcast_in_dim.36), channel_id=1, replica_groups=mesh['band'=16,'chip'=4,'core'=2] {'band','chip'}, dimensions={0} | all-to-all | bytes 5767168 | tf_op jit(solution)/shard_map/all_to_all | solution.py:466
  238.1 2.7 %collective-permute-start.4 = (bf16[11,512,256]{2,1,0:T(8,128)(2,1)S(1)}, bf16[11,512,256]{2,1,0:T(8,128)(2,1)S(1)}, u32[]{:S(2)}, u32[]{:S(2)}) collective-permute-start(bf16[11,512,256]{2,1,0:T(8,128)(2,1)S(1)} %bitcast.23), channel_id=1, source_target_pairs={{0,1},{1,0},{2,3},{3,2},{4,5},{5,4},{6,7},{7,6},{8,9},{9,8},{10,11... | collective-permute-start | bytes 8650760 | tf_op jit(solution)/shard_map/ppermute | solution.py:34
  240.8 2.5 %final_mine.1 = (f32[9,474,512]{2,1,0:T(8,128)}, f32[1,512]{1,0:T(1,128)}, f32[512,512]{1,0:T(8,128)}, f32[512,512]{1,0:T(8,128)}) custom-call(s32[1]{0:T(128)} %bitcast.6.half_ref, bf16[11,512,256]{2,1,0:T(8,128)(2,1)S(1)} %bitcast.24), custom_call_target="tpu_custom_call" | custom-call | bytes 9437184 | tf_op jit(solution)/shard_map/final_mine/pallas_call | solution.py:478
  243.3 2.4 collective-permute-done.4.sums_ref
  245.7 2.5 %final_other.1 = (f32[9,474,512]{2,1,0:T(8,128)}, f32[1,512]{1,0:T(1,128)}, f32[512,512]{1,0:T(8,128)}, f32[512,512]{1,0:T(8,128)}) custom-call(s32[1]{0:T(128)} %bitcast.5.half_ref, bf16[11,512,256]{2,1,0:T(8,128)(2,1)S(1)} %collective-permute-done.4.sums_ref, ...), custom_call_target="tpu_custom_call", output_to_operand_aliasing={{0}: (2, {}), {1}: (3, {}), {2}: (4, {}), {3}: (5, {})} | custom-call | bytes 9437184 | tf_op jit(solution)/shard_map/final_other/pallas_call | solution.py:478
  (84 shorter events, 25.2 us)
Async XLA Ops:
  0.6 48.5 %copy-start = (bf16[512,512]{1,0:T(8,128)(2,1)S(1)}, bf16[512,512]{1,0:T(8,128)(2,1)}, u32[]{:S(2)}) copy-start(bf16[512,512]{1,0:T(8,128)(2,1)} %param.13) | copy-start | bytes 1572868
  0.6 16.1 %copy-start.16 = (f32[512]{0:T(512)S(1)}, f32[512]{0:T(512)}, u32[]{:S(2)}) copy-start(f32[512]{0:T(512)} %param.11) | copy-start | bytes 6148
  1.4 15.2 %collective-permute-start.2 = (bf16[1,1,474]{2,1,0:T(2,128)(2,1)S(1)}, bf16[1,1,474]{2,1,0:T(2,128)(2,1)S(1)}, u32[]{:S(2)}, u32[]{:S(2)}) collective-permute-start(bf16[1,1,474]{2,1,0:T(2,128)(2,1)S(1)} %slice.11), channel_id=1, source_target_pairs={{0,9},{1,10},{2,11},{3,12},{4,13},{5,14},{6,15},{7,8},{8,17},{9,18... | collective-permute-start | bytes 2852 | tf_op jit(solution)/shard_map/ppermute | solution.py:330
  8.1 8.6 %collective-permute-start.1 = (bf16[1,64,474]{2,1,0:T(8,128)(2,1)S(1)}, bf16[1,64,474]{2,1,0:T(8,128)(2,1)S(1)}, u32[]{:S(2)}, u32[]{:S(2)}) collective-permute-start(bf16[1,64,474]{2,1,0:T(8,128)(2,1)S(1)} %slice.10), channel_id=1, source_target_pairs={{0,8},{8,16},{16,24},{24,32},{32,40},{40,48},{48,56},{56,64},{64,7... | collective-permute-start | bytes 182024 | tf_op jit(solution)/shard_map/ppermute | solution.py:329
  12.9 3.8 %collective-permute-start = (bf16[64,1,474]{2,1,0:T(2,128)(2,1)S(1)}, bf16[64,1,474]{2,1,0:T(2,128)(2,1)S(1)}, u32[]{:S(2)}, u32[]{:S(2)}) collective-permute-start(bf16[64,1,474]{2,1,0:T(2,128)(2,1)S(1)} %slice.9), channel_id=1, source_target_pairs={{0,1},{1,2},{2,3},{3,4},{4,5},{5,6},{6,7},{7,0},{8,9},{9,10},{10,1... | collective-permute-start | bytes 182024 | tf_op jit(solution)/shard_map/ppermute | solution.py:326
  37.4 9.4 %copy-start.24 = (s32[1,128,16]{1,2,0:T(8,128)S(1)}, s32[1,128,16]{1,2,0:T(8,128)}, u32[]{:S(2)}) copy-start(s32[1,128,16]{1,2,0:T(8,128)} %param.15) | copy-start | bytes 24580
  38.8 38.6 %copy-start.15 = (bf16[512,512]{1,0:T(8,128)(2,1)S(1)}, bf16[512,512]{1,0:T(8,128)(2,1)}, u32[]{:S(2)}) copy-start(bf16[512,512]{1,0:T(8,128)(2,1)} %w_ref.1) | copy-start | bytes 1572868
  38.8 38.6 %all-to-all-start = ((bf16[128,16,512]{2,1,0:T(8,128)(2,1)}), bf16[128,16,512]{2,1,0:T(8,128)(2,1)S(1)}, u32[]{:S(2)}, u32[]{:S(2)}) async-start(bf16[128,16,512]{2,1,0:T(8,128)(2,1)} %bitcast.28), calls=%async_computation | async-start | bytes 4194304 | tf_op jit(solution)/shard_map/all_to_all | solution.py:383
  77.3 14.4 %copy-start.4 = (bf16[128,16,512]{2,1,0:T(8,128)(2,1)}, bf16[128,16,512]{2,1,0:T(8,128)(2,1)S(1)}, u32[]{:S(2)}) copy-start(bf16[128,16,512]{2,1,0:T(8,128)(2,1)S(1)} %all-to-all-done) | copy-start | bytes 6291460
  77.3 2.0 copy-start.6
  90.4 7.0 %copy-start.23 = (s32[1,128,16]{2,1,0:T(8,128)S(1)}, s32[1,128,16]{2,1,0:T(8,128)}, u32[]{:S(2)}) copy-start(s32[1,128,16]{2,1,0:T(8,128)} %copy-done.22) | copy-start | bytes 24580
  91.7 35.7 %all-to-all-start.1 = ((bf16[128,16,512]{2,1,0:T(8,128)(2,1)}), bf16[128,16,512]{2,1,0:T(8,128)(2,1)}, u32[]{:S(2)}, u32[]{:S(2)}) async-start(bf16[128,16,512]{2,1,0:T(8,128)(2,1)} %bitcast.27), calls=%async_computation.1 | async-start | bytes 4194304 | tf_op jit(solution)/shard_map/all_to_all | solution.py:415
  101.3 7.0 %copy-start.20 = (bf16[2048,512]{1,0:T(8,128)(2,1)S(1)}, bf16[2048,512]{1,0:T(8,128)(2,1)}, u32[]{:S(2)}) copy-start(bf16[2048,512]{1,0:T(8,128)(2,1)} %copy-done.19) | copy-start | bytes 6291460
  104.6 3.6 %copy-start.2 = (bf16[9,512,1024]{2,1,0:T(8,128)(2,1)}, bf16[9,512,1024]{2,1,0:T(8,128)(2,1)S(1)}, u32[]{:S(2)}) copy-start(bf16[9,512,1024]{2,1,0:T(8,128)(2,1)S(1)} %flip.1.patches_hbm) | copy-start | bytes 28311556
  108.3 1.9 copy-start.21
  108.3 2.4 copy-start.5
  108.3 2.5 copy-start.18
  110.7 34.4 %slice-start = ((s8[9437184]{0:T(1024)(128)(4,1)}), s8[1048576]{0:T(1024)(128)(4,1)S(1)}, s32[]{:S(2)}) async-start(s8[9437184]{0:T(1024)(128)(4,1)} %bitcast.21), calls=%async_computation.4 | async-start | bytes 2097152
  127.5 3.7 %copy-start.3 = (bf16[9,512,1024]{2,1,0:T(8,128)(2,1)S(1)}, bf16[9,512,1024]{2,1,0:T(8,128)(2,1)}, u32[]{:S(2)}) copy-start(bf16[9,512,1024]{2,1,0:T(8,128)(2,1)} %copy-done.2) | copy-start | bytes 28311556
  132.7 12.4 %slice-start.1 = ((s8[9437184]{0:T(1024)(128)(4,1)}), s8[4194304]{0:T(1024)(128)(4,1)S(1)}, s32[]{:S(2)}) async-start(s8[9437184]{0:T(1024)(128)(4,1)} %bitcast.21), calls=%async_computation.5 | async-start | bytes 8388608
  132.7 12.4 %slice-start.2 = ((s8[9437184]{0:T(1024)(128)(4,1)}), s8[4194304]{0:T(1024)(128)(4,1)S(1)}, s32[]{:S(2)}) async-start(s8[9437184]{0:T(1024)(128)(4,1)} %bitcast.21), calls=%async_computation.6 | async-start | bytes 8388608
  143.9 8.3 %collective-permute-start.3 = (bf16[11,512,256]{2,1,0:T(8,128)(2,1)S(1)}, bf16[11,512,256]{2,1,0:T(8,128)(2,1)S(1)}, u32[]{:S(2)}, u32[]{:S(2)}) collective-permute-start(bf16[11,512,256]{2,1,0:T(8,128)(2,1)S(1)} %get-tuple-element.36), channel_id=1, source_target_pairs={{0,1},{1,0},{2,3},{3,2},{4,5},{5,4},{6,7},{7,6},{8,9},{9,8},{10,11... | collective-permute-start | bytes 8650760 | tf_op jit(solution)/shard_map/ppermute | solution.py:34
  238.1 7.6 %collective-permute-start.4 = (bf16[11,512,256]{2,1,0:T(8,128)(2,1)S(1)}, bf16[11,512,256]{2,1,0:T(8,128)(2,1)S(1)}, u32[]{:S(2)}, u32[]{:S(2)}) collective-permute-start(bf16[11,512,256]{2,1,0:T(8,128)(2,1)S(1)} %bitcast.23), channel_id=1, source_target_pairs={{0,1},{1,0},{2,3},{3,2},{4,5},{5,4},{6,7},{7,6},{8,9},{9,8},{10,11... | collective-permute-start | bytes 8650760 | tf_op jit(solution)/shard_map/ppermute | solution.py:34
  245.7 2.6 %copy-start.1 = (bf16[512,512]{1,0:T(8,128)(2,1)S(1)}, bf16[512,512]{1,0:T(8,128)(2,1)}, u32[]{:S(2)}) copy-start(bf16[512,512]{1,0:T(8,128)(2,1)} %param.13) | copy-start | bytes 1572868
  (11 other events, 16.0 us)
